TPU v7x, 128 devices: a whole 4x4x4 slice. The times are simulated.
128 devices in a mesh: group: 2 (over x_lo), sample: 16 (over z, x_hi, core), tensor: 4 (over y).
Axes of the slice: x: 4 (x_hi: 2, x_lo: 2; x = x_hi * 2 + x_lo), y: 4, z: 4, core: 2. Of those that a mesh axis runs over, the one named last changes fastest.
Arguments:
- resp_hidden: bfloat16 [32, 512, 5120], P(('group', 'sample')), parts along dimension 0, may hold values from -6 to 6
- prompt_hidden: bfloat16 [16384, 5120], P(('group', 'sample')), parts along dimension 0, may hold values from -6 to 6
- lengths: int32 [32], P(('group', 'sample')), parts along dimension 0, may hold values from 1 to 512, 5120 in all
- norm_gain: bfloat16 [5120], replicated, may hold values from 0.099609375 to 1.8984375
- wq: bfloat16 [5120, 2560], P('sample', 'tensor'), may hold values from -0.078125 to 0.078125
- wk: bfloat16 [5120, 512], P('sample', 'tensor'), may hold values from -0.078125 to 0.078125
- wv: bfloat16 [5120, 512], P('sample', 'tensor'), may hold values from -0.078125 to 0.078125
- q_bias: bfloat16 [2560], P('tensor'), may hold values from -12 to 12
- k_bias: bfloat16 [512], P('tensor'), may hold values from -12 to 12
- value_bias: bfloat16 [512], P('tensor'), may hold values from -3 to 3
- wo_t: bfloat16 [5120, 2560], P('sample', 'tensor'), may hold values from -0.5 to 0.5
- post_gain: bfloat16 [5120], replicated, may hold values from 0.099609375 to 1.8984375
Outputs:
- mixed: bfloat16 [32, 512, 5120], P(('group', 'sample')), parts along dimension 0
There are 2 independent parts, one for each index of `group`. A program takes and returns all parts, laid end to end along the dimension named above; an argument that names none is the same for every part. Nothing has to cross between parts.
Inputs may be any that keep to these rules, and one draw needn't show every extreme that they name: The 16 lengths of each group sum to 5120 (the whole array, all groups together, sums to that times the number of groups); the longest response of each group has exactly 512 tokens.
All inputs are finite; a program needn't handle non-finite values.
Results may differ from a plain program's by a relative error of at most 0.017.
The roundings to bfloat16 on the way count: a program that leaves them out, or rounds other values in their place, can miss the bound.
Values may be sent and summed in bfloat16 or wider, within the bound.
A program may use at most 128 MiB of HBM per device.

v0:
```python
import math

import jax
import jax.numpy as jnp
from jax import lax
from jax.sharding import PartitionSpec as P

HEAD_SIZE = 128


EPS = 1e-06
THETA = 1000000.0


def normalize(rows, gain):
    values = rows.astype(jnp.float32)
    meansq = jnp.mean(values * values, axis=-1, keepdims=True)
    return values * lax.rsqrt(meansq + EPS) * gain.astype(jnp.float32)


def rotary_embed(values, positions):
    half = values.shape[-1] // 2
    lanes = jnp.arange(half).astype(jnp.float32)
    inverse = THETA ** (-2.0 * lanes / values.shape[-1])
    angle = positions[:, None] * inverse[None, :]
    cosine = jnp.cos(angle)[:, None, :]
    sine = jnp.sin(angle)[:, None, :]
    first_half = values[..., :half]
    second_half = values[..., half:]
    return jnp.concatenate(
        [first_half * cosine - second_half * sine, second_half * cosine + first_half * sine],
        axis=-1,
    )


def add_rows(left, piece):
    return jnp.dot(left, piece, preferred_element_type=jnp.float32)


def absorb(score, block_values, state):
    highest, running, weighted = state
    fresh = jnp.maximum(highest, jnp.max(score, axis=-1))
    rescale = jnp.exp(highest - fresh)
    expd = jnp.exp(score - fresh[:, None])
    running = running * rescale + jnp.sum(expd, axis=-1)
    weighted = weighted * rescale[:, None] + jnp.dot(
        expd.astype(jnp.bfloat16), block_values, preferred_element_type=jnp.float32
    )
    return (fresh, running, weighted)


def project_heads(attended, wo_t):
    return jnp.einsum(
        "rk,dk->rd",
        attended,
        lax.all_gather(wo_t, "sample", axis=0, tiled=True),
        preferred_element_type=jnp.float32,
    )


def on_device(
    resp_hidden,
    prompt_hidden,
    lengths,
    norm_gain,
    wq,
    wk,
    wv,
    q_bias,
    k_bias,
    value_bias,
    wo_t,
    post_gain,
):
    f32 = jnp.float32
    to_brain_float = jnp.bfloat16
    resp = resp_hidden[0]
    rows = resp.shape[0]
    prompt_rows = prompt_hidden.shape[0]
    q_cols = wq.shape[1]
    kv_cols = wk.shape[1]
    q_heads = q_cols // HEAD_SIZE
    kv_heads = kv_cols // HEAD_SIZE
    prefix_share = q_heads // kv_heads
    owner = lax.axis_index("sample")
    resp_normed = normalize(resp, norm_gain).astype(to_brain_float)
    prompt_normed = normalize(prompt_hidden, norm_gain).astype(to_brain_float)
    stacked = jnp.concatenate([resp_normed, prompt_normed], 0)
    q_raw = add_rows(resp_normed, lax.all_gather(wq, "sample", axis=0, tiled=True))
    pieces = (
        lax.all_gather(wk, "sample", axis=0, tiled=True),
        lax.all_gather(wv, "sample", axis=0, tiled=True),
    )
    k_raw = add_rows(stacked, pieces[0])
    v_raw = add_rows(stacked, pieces[1])
    response_positions = (prompt_rows * lax.axis_size("sample") + jnp.arange(rows)).astype(f32)
    prompt_positions = (owner * prompt_rows + jnp.arange(prompt_rows)).astype(f32)
    all_pos = jnp.concatenate([response_positions, prompt_positions], 0)
    queries = rotary_embed(
        (q_raw + q_bias.astype(f32)).reshape(rows, q_heads, HEAD_SIZE), response_positions
    ).astype(to_brain_float)
    keys_all = rotary_embed(
        (k_raw + k_bias.astype(f32)).reshape(rows + prompt_rows, kv_heads, HEAD_SIZE), all_pos
    ).astype(to_brain_float)
    values_all = (
        (v_raw + value_bias.astype(f32))
        .astype(to_brain_float)
        .reshape(rows + prompt_rows, kv_heads, HEAD_SIZE)
    )
    own_keys = keys_all[:rows].transpose(1, 0, 2)
    own_values = values_all[:rows].transpose(1, 0, 2)
    prompt_key_rows = keys_all[rows:].reshape(prompt_rows, kv_cols)
    prompt_value_rows = values_all[rows:].reshape(prompt_rows, kv_cols)
    scale = 1.0 / math.sqrt(HEAD_SIZE)
    width = min(512, rows)
    per_head = prefix_share * rows // width
    nblocks = kv_heads * per_head
    qblocks = queries.transpose(1, 0, 2)
    block_heads = jnp.arange(nblocks) // per_head
    block_rows = (jnp.arange(nblocks)[:, None] * width + jnp.arange(width)[None, :]) % rows
    initial = (
        jnp.full((nblocks, width), -jnp.inf, f32),
        jnp.zeros((nblocks, width), f32),
        jnp.zeros((nblocks, width, HEAD_SIZE), f32),
    )
    pieces = (
        lax.all_gather(prompt_key_rows, "sample", axis=0, tiled=True),
        lax.all_gather(prompt_value_rows, "sample", axis=0, tiled=True),
    )
    piece_keys = pieces[0].reshape(-1, kv_heads, HEAD_SIZE).transpose(1, 0, 2)
    piece_values = pieces[1].reshape(-1, kv_heads, HEAD_SIZE).transpose(1, 0, 2)

    def one_block(args):
        block_q, head, highest, running, weighted = args
        keys = lax.dynamic_index_in_dim(piece_keys, head, 0, keepdims=False)
        values = lax.dynamic_index_in_dim(piece_values, head, 0, keepdims=False)
        score = jnp.einsum("qd,kd->qk", block_q, keys, preferred_element_type=f32) * scale
        return absorb(score, values, (highest, running, weighted))

    state = lax.map(one_block, (qblocks, block_heads) + tuple(initial))
    key_index = jnp.arange(rows)

    def self_block(args):
        block_q, head, positions, highest, running, weighted = args
        keys = lax.dynamic_index_in_dim(own_keys, head, 0, keepdims=False)
        values = lax.dynamic_index_in_dim(own_values, head, 0, keepdims=False)
        score = jnp.einsum("qd,kd->qk", block_q, keys, preferred_element_type=f32) * scale
        score = jnp.where(key_index[None, :] <= positions[:, None], score, -jnp.inf)
        return absorb(score, values, (highest, running, weighted))

    highest, running, weighted = lax.map(
        self_block, (qblocks, block_heads, block_rows) + tuple(state)
    )
    heads_out = (weighted / running[..., None]).transpose(1, 0, 2).reshape(rows, q_cols)
    live = (jnp.arange(rows) < lengths[0])[:, None]
    attended = jnp.where(live, heads_out, 0.0).astype(to_brain_float)
    terms = project_heads(attended, wo_t)
    whole_sum = lax.psum(terms.astype(jnp.bfloat16), "tensor").astype(jnp.float32)
    resid = resp.astype(f32) + whole_sum
    mixed = jnp.where(live, normalize(resid, post_gain), 0.0).astype(to_brain_float)
    return mixed[None]


def solution(mesh):
    placed = (
        P(("group", "sample"), None, None),
        P(("group", "sample"), None),
        P(("group", "sample")),
        P(),
        P("sample", "tensor"),
        P("sample", "tensor"),
        P("sample", "tensor"),
        P("tensor"),
        P("tensor"),
        P("tensor"),
        P("sample", "tensor"),
        P(),
    )
    return jax.shard_map(
        on_device,
        mesh=mesh,
        in_specs=placed,
        out_specs=P(("group", "sample"), None, None),
        check_vma=False,
    )
```

profile of v0, /device:TPU:1, one launch (start us, length us, event | category | flops | bytes accessed | tf_op | source)
XLA Modules:
  0.0 529.5 jit_solution(5036690060676875883)
XLA Ops:
  8.1 3.7 fusion.42
  13.3 12.5 %fusion.44 = (bf16[512,5120]{1,0:T(8,128)(2,1)}, bf16[512,5120]{1,0:T(8,128)(2,1)}) fusion(bf16[512,5120]{1,0:T(8,128)(2,1)} %param.17, f32[512]{0:T(512)S(1)} %get-tuple-element.259, f32[5120]{0:T(1024)S(1)} %convert_element_type.101, f32[512]{0:T(512)S(1)} %get-tuple-element.260, bf16[1,512,5120]{2,1,0:T(8,128)(2,1)} %param.16), kind=kLoop, calls=%fused_computation.48 | loop fusion | flops 20971520 | bytes 20996096 | tf_op jit(solution)/shard_map/convert_element_type | solution.py:87
  25.8 33.3 %all-gather.10.cloned.1.call-done = bf16[5120,128]{1,0:T(8,128)(2,1)} async-done(((bf16[320,128]{1,0:T(8,128)(2,1)}), bf16[5120,128]{1,0:T(8,128)(2,1)}) %all-gather.10.cloned.1.call-update) | async-done | bytes 1310736 | tf_op jit(solution)/shard_map/all_gather | solution.py:91
  59.1 8.0 %fusion.53 = f32[1024,1,128]{0,2,1:T(8,128)S(1)} fusion(bf16[5120,128]{1,0:T(8,128)(2,1)} %all-gather.10.cloned.1.call-done, bf16[512,5120]{1,0:T(8,128)(2,1)} %get-tuple-element.255, bf16[512,5120]{1,0:T(8,128)(2,1)} %get-tuple-element.256, f32[128]{0:T(128)S(1)} %convert_element_type.108), kind=kOutput, calls=%fused_computation.63 | convolution fusion | flops 1363279872 | bytes 12321280 | tf_op jit(solution)/shard_map/dot_general | solution.py:37
  69.8 36.2 %all-gather.12.cloned.1.call-done = bf16[5120,128]{1,0:T(8,128)(2,1)} async-done(((bf16[320,128]{1,0:T(8,128)(2,1)}), bf16[5120,128]{1,0:T(8,128)(2,1)}) %all-gather.12.cloned.1.call-update) | async-done | bytes 1310736 | tf_op jit(solution)/shard_map/all_gather | solution.py:92
  105.9 7.3 %fusion.55 = bf16[1024,128]{1,0:T(8,128)(2,1)S(1)} fusion(bf16[5120,128]{1,0:T(8,128)(2,1)} %all-gather.12.cloned.1.call-done, bf16[512,5120]{1,0:T(8,128)(2,1)} %get-tuple-element.255, bf16[512,5120]{1,0:T(8,128)(2,1)} %get-tuple-element.256, f32[128]{0:T(128)S(1)} %convert_element_type.110), kind=kOutput, calls=%fused_computation.65 | convolution fusion | flops 1363410944 | bytes 12059136 | tf_op jit(solution)/shard_map/dot_general | solution.py:37
  117.8 36.4 %all-gather.18.cloned.1.call-done = bf16[8192,1,128]{0,2,1:T(8,128)(2,1)} async-done(((bf16[512,1,128]{0,2,1:T(8,128)(2,1)}), bf16[8192,1,128]{0,2,1:T(8,128)(2,1)}) %all-gather.18.cloned.1.call-update) | async-done | bytes 2097168 | tf_op jit(solution)/shard_map/all_gather | solution.py:127
  154.2 3.2 copy.19
  157.5 62.6 %all-gather.8.cloned.1.call-done = bf16[5120,640]{1,0:T(8,128)(2,1)} async-done(((bf16[320,640]{1,0:T(8,128)(2,1)}), bf16[5120,640]{1,0:T(8,128)(2,1)}) %all-gather.8.cloned.1.call-update) | async-done | bytes 6553616 | tf_op jit(solution)/shard_map/all_gather | solution.py:89
  220.0 9.8 %convolution_add_fusion.1 = f32[512,640]{1,0:T(8,128)} fusion(bf16[512,5120]{1,0:T(8,128)(2,1)} %get-tuple-element.256, bf16[5120,640]{1,0:T(8,128)(2,1)} %all-gather.8.cloned.1.call-done, f32[640]{0:T(1024)S(1)} %convert_element_type.103), kind=kOutput, calls=%fused_computation.59 | convolution fusion | flops 3355770880 | bytes 13109760 | tf_op jit(solution)/shard_map/dot_general | solution.py:37
  235.1 32.6 %all-gather.14.cloned.1.call-done = bf16[8192,128]{1,0:T(8,128)(2,1)} async-done(((bf16[512,128]{1,0:T(8,128)(2,1)}), bf16[8192,128]{1,0:T(8,128)(2,1)}) %all-gather.14.cloned.1.call-update) | async-done | bytes 2097168 | tf_op jit(solution)/shard_map/all_gather | solution.py:128
  267.7 107.0 %while.29 = (s32[]{:T(128)}, f32[5,512]{1,0:T(8,128)S(1)}, f32[5,512]{1,0:T(8,128)S(1)}, f32[5,512,128]{2,1,0:T(8,128)}, bf16[5,512,128]{2,1,0:T(8,128)(2,1)S(1)...) while((s32[]{:T(128)}, f32[5,512]{1,0:T(8,128)S(1)}, ...), condition=%wide.region_5.6_spmd, body=%wide.region_2.5_spmd.sunk | while | flops 2181105152 | bytes 130445976 | solution.py:140
  270.2 5.7 %copy-done = f32[512,8192]{1,0:T(8,128)} copy-done((f32[512,8192]{1,0:T(8,128)}, f32[512,8192]{1,0:T(8,128)S(1)}, u32[]{:S(2)}) %copy-start) | copy-done | bytes 16777240 | tf_op jit(solution)/shard_map/while
  275.9 4.2 fusion.92
  280.1 8.6 %fusion.91 = f32[512]{0:T(512)S(1)} fusion(f32[512,8192]{1,0:T(8,128)} %copy-done, f32[512]{0:T(512)S(1)} %get-tuple-element.363), kind=kLoop, calls=%fused_computation.4.clone.1 | loop fusion | flops 12582400 | bytes 16781312 | tf_op jit(solution)/shard_map/while/body/eval_jaxpr/reduce_sum | solution.py:45
  291.4 5.7 %copy-done = f32[512,8192]{1,0:T(8,128)} copy-done((f32[512,8192]{1,0:T(8,128)}, f32[512,8192]{1,0:T(8,128)S(1)}, u32[]{:S(2)}) %copy-start) | copy-done | bytes 16777240 | tf_op jit(solution)/shard_map/while
  297.1 4.2 fusion.92
  301.3 9.4 %fusion.91 = f32[512]{0:T(512)S(1)} fusion(f32[512,8192]{1,0:T(8,128)} %copy-done, f32[512]{0:T(512)S(1)} %get-tuple-element.363), kind=kLoop, calls=%fused_computation.4.clone.1 | loop fusion | flops 12582400 | bytes 16781312 | tf_op jit(solution)/shard_map/while/body/eval_jaxpr/reduce_sum | solution.py:45
  313.3 5.7 %copy-done = f32[512,8192]{1,0:T(8,128)} copy-done((f32[512,8192]{1,0:T(8,128)}, f32[512,8192]{1,0:T(8,128)S(1)}, u32[]{:S(2)}) %copy-start) | copy-done | bytes 16777240 | tf_op jit(solution)/shard_map/while
  319.1 4.2 fusion.92
  323.3 8.9 %fusion.91 = f32[512]{0:T(512)S(1)} fusion(f32[512,8192]{1,0:T(8,128)} %copy-done, f32[512]{0:T(512)S(1)} %get-tuple-element.363), kind=kLoop, calls=%fused_computation.4.clone.1 | loop fusion | flops 12582400 | bytes 16781312 | tf_op jit(solution)/shard_map/while/body/eval_jaxpr/reduce_sum | solution.py:45
  334.8 5.7 %copy-done = f32[512,8192]{1,0:T(8,128)} copy-done((f32[512,8192]{1,0:T(8,128)}, f32[512,8192]{1,0:T(8,128)S(1)}, u32[]{:S(2)}) %copy-start) | copy-done | bytes 16777240 | tf_op jit(solution)/shard_map/while
  340.5 4.2 fusion.92
  344.8 8.6 %fusion.91 = f32[512]{0:T(512)S(1)} fusion(f32[512,8192]{1,0:T(8,128)} %copy-done, f32[512]{0:T(512)S(1)} %get-tuple-element.363), kind=kLoop, calls=%fused_computation.4.clone.1 | loop fusion | flops 12582400 | bytes 16781312 | tf_op jit(solution)/shard_map/while/body/eval_jaxpr/reduce_sum | solution.py:45
  356.0 5.7 %copy-done = f32[512,8192]{1,0:T(8,128)} copy-done((f32[512,8192]{1,0:T(8,128)}, f32[512,8192]{1,0:T(8,128)S(1)}, u32[]{:S(2)}) %copy-start) | copy-done | bytes 16777240 | tf_op jit(solution)/shard_map/while
  361.7 4.2 fusion.92
  365.9 8.6 %fusion.91 = f32[512]{0:T(512)S(1)} fusion(f32[512,8192]{1,0:T(8,128)} %copy-done, f32[512]{0:T(512)S(1)} %get-tuple-element.363), kind=kLoop, calls=%fused_computation.4.clone.1 | loop fusion | flops 12582400 | bytes 16781312 | tf_op jit(solution)/shard_map/while/body/eval_jaxpr/reduce_sum | solution.py:45
  374.8 14.4 %while.30 = (s32[]{:T(128)}, f32[5,512]{1,0:T(8,128)S(1)}, f32[5,512,128]{1,2,0:T(8,128)}, f32[5,512]{1,0:T(8,128)S(1)}, f32[5,512]{1,0:T(8,128)S(1)}, /*index=5...) while((s32[]{:T(128)}, f32[5,512]{1,0:T(8,128)S(1)}, ...), condition=%wide.region_9.10_spmd.clone, body=%wide.region_6.9_spmd.clone.sunk | while | flops 136448000 | bytes 5155469 | solution.py:151
  390.8 9.0 %convolution_convert_fusion = bf16[512,5120]{1,0:T(8,128)(2,1)} fusion(bf16[512,640]{0,1:T(8,128)(2,1)S(1)} %fusion.51, bf16[5120,640]{1,0:T(8,128)(2,1)} %all-gather.16.cloned.1.call-done), kind=kOutput, calls=%fused_computation.55 | convolution fusion | flops 3358064640 | bytes 12451840 | tf_op jit(solution)/shard_map/rk,dk->rd/dot_general | solution.py:53
  400.5 108.1 %all-reduce.2.cloned.1.call-done = bf16[512,5120]{1,0:T(8,128)(2,1)} async-done(((bf16[512,5120]{1,0:T(8,128)(2,1)}), bf16[512,5120]{1,0:T(8,128)(2,1)}) %all-reduce.2.cloned.1.call-update) | async-done | bytes 5242896 | tf_op jit(solution)/shard_map/psum | solution.py:158
  508.6 6.0 %multiply_reduce_fusion.1 = f32[512]{0:T(512)S(1)} fusion(bf16[512,5120]{1,0:T(8,128)(2,1)} %all-reduce.2.cloned.1.call-done, bf16[1,512,5120]{2,1,0:T(8,128)(2,1)} %param.16), kind=kLoop, calls=%fused_computation.54 | loop fusion | flops 13106688 | bytes 10487808 | tf_op jit(solution)/shard_map/reduce_sum | solution.py:17
  514.6 8.1 %fusion.50 = bf16[1,512,5120]{2,1,0:T(8,128)(2,1)} fusion(bf16[512,5120]{1,0:T(8,128)(2,1)S(1)} %copy-done.3, bf16[1,512,5120]{2,1,0:T(8,128)(2,1)} %param.16, f32[5120]{0:T(1024)S(1)} %convert_element_type.115, f32[512]{0:T(512)S(1)} %add_rsqrt_fusion, pred[512]{0:T(512)(128)(4,1)S(1)} %copy-done.7), kind=kLoop, calls=%fused_computation.58 | loop fusion | flops 18350080 | bytes 15751680 | tf_op jit(solution)/shard_map/broadcast_in_dim | solution.py:161
  (153 shorter events, 43.9 us)
Async XLA Ops:
  6.5 52.5 %all-gather.10.cloned.1.call-start = ((), (), s32[]{:S(2)}) async-start(), calls=%async_computation.1 | async-start | bytes 1392640 | tf_op jit(solution)/shard_map/all_gather | solution.py:91
  7.3 98.7 %all-gather.12.cloned.1.call-start = ((), (), s32[]{:S(2)}) async-start(), calls=%async_computation.2 | async-start | bytes 1392640 | tf_op jit(solution)/shard_map/all_gather | solution.py:92
  8.0 146.2 %all-gather.18.cloned.1.call-start = ((), (), s32[]{:S(2)}) async-start(), calls=%async_computation.6 | async-start | bytes 2228224 | tf_op jit(solution)/shard_map/all_gather | solution.py:127
  8.1 4.0 copy-start.1
  8.1 5.1 copy-start.5
  8.1 5.1 copy-start.9
  59.1 10.6 %copy-start.10 = (bf16[128]{0:T(256)(128)(2,1)S(1)}, bf16[128]{0:T(256)(128)(2,1)}, u32[]{:S(2)}) copy-start(bf16[128]{0:T(256)(128)(2,1)} %param.25) | copy-start | bytes 772
  68.9 151.1 %all-gather.8.cloned.1.call-start = ((), (), s32[]{:S(2)}) async-start(), calls=%async_computation | async-start | bytes 6963200 | tf_op jit(solution)/shard_map/all_gather | solution.py:89
  69.5 198.2 %all-gather.14.cloned.1.call-start = ((), (), s32[]{:S(2)}) async-start(), calls=%async_computation.3 | async-start | bytes 2228224 | tf_op jit(solution)/shard_map/all_gather | solution.py:128
  69.7 46.0 %copy-start.8 = (bf16[640]{0:T(1024)(128)(2,1)S(1)}, bf16[640]{0:T(1024)(128)(2,1)}, u32[]{:S(2)}) copy-start(bf16[640]{0:T(1024)(128)(2,1)} %param.23) | copy-start | bytes 3844
  113.9 277.0 %all-gather.16.cloned.1.call-start = ((), (), s32[]{:S(2)}) async-start(), calls=%async_computation.4 | async-start | bytes 6963200 | tf_op jit(solution)/shard_map/all_gather | solution.py:56
  114.5 394.1 %all-reduce.2.cloned.1.call-start = ((), (), s32[]{:S(2)}) async-start(), calls=%async_computation.5 | async-start | bytes 10485760 | tf_op jit(solution)/shard_map/psum | solution.py:158
  267.7 107.0 %copy-start.4 = (bf16[1,512,128]{2,1,0:T(8,128)(2,1)S(1)}, bf16[1,512,128]{2,1,0:T(8,128)(2,1)}, u32[]{:S(2)}) copy-start(bf16[1,512,128]{2,1,0:T(8,128)(2,1)} %copy.21) | copy-start | bytes 393220
  267.7 8.2 %copy-start.2 = (bf16[1,8192,128]{2,1,0:T(8,128)(2,1)S(1)}, bf16[1,8192,128]{2,1,0:T(8,128)(2,1)}, u32[]{:S(2)}) copy-start(bf16[1,8192,128]{2,1,0:T(8,128)(2,1)} %get-tuple-element.403) | copy-start | bytes 6291460 | tf_op jit(solution)/shard_map/while
  270.1 5.7 %copy-start = (f32[512,8192]{1,0:T(8,128)}, f32[512,8192]{1,0:T(8,128)S(1)}, u32[]{:S(2)}) copy-start(f32[512,8192]{1,0:T(8,128)S(1)} %get-tuple-element.364) | copy-start | bytes 50331652 | tf_op jit(solution)/shard_map/while
  288.9 8.2 %copy-start.2 = (bf16[1,8192,128]{2,1,0:T(8,128)(2,1)S(1)}, bf16[1,8192,128]{2,1,0:T(8,128)(2,1)}, u32[]{:S(2)}) copy-start(bf16[1,8192,128]{2,1,0:T(8,128)(2,1)} %get-tuple-element.403) | copy-start | bytes 6291460 | tf_op jit(solution)/shard_map/while
  291.3 5.7 %copy-start = (f32[512,8192]{1,0:T(8,128)}, f32[512,8192]{1,0:T(8,128)S(1)}, u32[]{:S(2)}) copy-start(f32[512,8192]{1,0:T(8,128)S(1)} %get-tuple-element.364) | copy-start | bytes 50331652 | tf_op jit(solution)/shard_map/while
  310.9 8.2 %copy-start.2 = (bf16[1,8192,128]{2,1,0:T(8,128)(2,1)S(1)}, bf16[1,8192,128]{2,1,0:T(8,128)(2,1)}, u32[]{:S(2)}) copy-start(bf16[1,8192,128]{2,1,0:T(8,128)(2,1)} %get-tuple-element.403) | copy-start | bytes 6291460 | tf_op jit(solution)/shard_map/while
  313.3 5.7 %copy-start = (f32[512,8192]{1,0:T(8,128)}, f32[512,8192]{1,0:T(8,128)S(1)}, u32[]{:S(2)}) copy-start(f32[512,8192]{1,0:T(8,128)S(1)} %get-tuple-element.364) | copy-start | bytes 50331652 | tf_op jit(solution)/shard_map/while
  332.4 8.2 %copy-start.2 = (bf16[1,8192,128]{2,1,0:T(8,128)(2,1)S(1)}, bf16[1,8192,128]{2,1,0:T(8,128)(2,1)}, u32[]{:S(2)}) copy-start(bf16[1,8192,128]{2,1,0:T(8,128)(2,1)} %get-tuple-element.403) | copy-start | bytes 6291460 | tf_op jit(solution)/shard_map/while
  334.8 5.7 %copy-start = (f32[512,8192]{1,0:T(8,128)}, f32[512,8192]{1,0:T(8,128)S(1)}, u32[]{:S(2)}) copy-start(f32[512,8192]{1,0:T(8,128)S(1)} %get-tuple-element.364) | copy-start | bytes 50331652 | tf_op jit(solution)/shard_map/while
  353.5 8.2 %copy-start.2 = (bf16[1,8192,128]{2,1,0:T(8,128)(2,1)S(1)}, bf16[1,8192,128]{2,1,0:T(8,128)(2,1)}, u32[]{:S(2)}) copy-start(bf16[1,8192,128]{2,1,0:T(8,128)(2,1)} %get-tuple-element.403) | copy-start | bytes 6291460 | tf_op jit(solution)/shard_map/while
  356.0 5.7 %copy-start = (f32[512,8192]{1,0:T(8,128)}, f32[512,8192]{1,0:T(8,128)S(1)}, u32[]{:S(2)}) copy-start(f32[512,8192]{1,0:T(8,128)S(1)} %get-tuple-element.364) | copy-start | bytes 50331652 | tf_op jit(solution)/shard_map/while
  374.7 15.9 %copy-start.7 = (pred[512]{0:T(512)(128)(4,1)S(1)}, pred[512]{0:T(512)(128)(4,1)}, u32[]{:S(2)}) copy-start(pred[512]{0:T(512)(128)(4,1)} %iota_compare_fusion.1) | copy-start | bytes 1540
  399.8 0.7 copy-start.6
  508.6 6.0 %copy-start.3 = (bf16[512,5120]{1,0:T(8,128)(2,1)S(1)}, bf16[512,5120]{1,0:T(8,128)(2,1)}, u32[]{:S(2)}) copy-start(bf16[512,5120]{1,0:T(8,128)(2,1)} %all-reduce.2.cloned.1.call-done) | copy-start | bytes 15728644
Sparse Core Ops, SparseCore 0:
  9.8 49.2 all-gather.9
  61.5 44.3 all-gather.11
  108.3 45.9 all-gather.17
  156.6 63.4 all-gather.7
  222.3 45.3 all-gather.13
  270.0 64.1 all-gather.15
  400.0 108.5 all-reduce.1
where the time goes:
time: 530 us
  waiting for transfers between devices  312 us (59%)
  other arithmetic  84.3 us (16%)
  matrix products  75.3 us (14%)
  local copies, waits for them, and re-layouts  42.7 us (8%)
  between operations  14.4 us (3%)
    psum x1, waiting for transfers between devices, on_device(): lax.psum(terms.astype(jnp.bfloat16), 'tensor').astype(jnp.float32)  108 us
    all_gather x1, waiting for transfers between devices, on_device(): lax.all_gather(wq, 'sample', axis=0, tiled=True)  62.6 us
    reduce_sum x10, other arithmetic, absorb(): running = running * rescale + jnp.sum(expd, axis=-1)  45.2 us
    all_gather x1, waiting for transfers between devices, on_device(): lax.all_gather(prompt_key_rows, 'sample', axis=0, tiled=True)  36.4 us
    all_gather x1, waiting for transfers between devices, on_device(): lax.all_gather(wv, 'sample', axis=0, tiled=True)  36.2 us
    all_gather x1, waiting for transfers between devices, on_device(): lax.all_gather(wk, 'sample', axis=0, tiled=True)  33.3 us
    all_gather x1, waiting for transfers between devices, on_device(): lax.all_gather(prompt_value_rows, 'sample', axis=0, tiled=True)  32.6 us
    while x20, local copies, waits for them, and re-layouts  28.6 us
  transfers between devices with their start and end apart: 7, of which 6 were waited for; matrix products, arithmetic and copies ran while one was open for 28% of the time, Pallas kernels for 0%

commit v1 on v0

v1 whole, which is shorter than its diff:
```python
import math

import jax
import jax.numpy as jnp
import numpy as np
from jax import lax
from jax.experimental import pallas as pl
from jax.experimental.pallas import tpu as pltpu
from jax.sharding import PartitionSpec as P

HEAD = 128
EPS = 1e-06
THETA = 1000000.0
WIDTH = 5120
ROWS = 512
Q_HEADS = 5
Q_COLS = Q_HEADS * HEAD
F32 = jnp.float32
BF16 = jnp.bfloat16
NT = (((1,), (1,)), ((), ()))
ALL = slice(None)


def rope_tables():
    half = np.arange(HEAD // 2, dtype=np.float64)
    inverse = THETA ** (-2.0 * half / HEAD)

    def pair(positions):
        angle = positions[:, None] * inverse[None, :]
        cosine, sine = np.cos(angle), np.sin(angle)
        both = np.concatenate([cosine, cosine], 1), np.concatenate([sine, sine], 1)
        return both[0].astype(np.float32), both[1].astype(np.float32)

    return pair(np.arange(ROWS, dtype=np.float64)) + pair(np.arange(24, dtype=np.float64) * ROWS)


class Net:
    def __init__(self, send, recv, core_send, core_recv, sibling):
        self.send, self.recv, self.core_send, self.core_recv = send, recv, core_send, core_recv
        self.sibling = sibling
        self.count = 0
        self.sent = []

    def describe(self, region, i, peer):
        ref = region()
        return pltpu.make_async_remote_copy(
            src_ref=ref, dst_ref=ref, send_sem=self.send.at[i], recv_sem=self.recv.at[i],
            device_id=peer, device_id_type=pl.DeviceIdType.MESH)

    def put(self, region, peer):
        i = self.count
        self.count += 1
        self.describe(region, i, peer).start()
        self.sent.append((region, i, peer))
        return i

    def got(self, region, i):
        self.describe(region, i, self.sibling).wait_recv()

    def core(self, region, k):
        ref = region()
        return pltpu.make_async_remote_copy(
            src_ref=ref, dst_ref=ref, send_sem=self.core_send.at[k], recv_sem=self.core_recv.at[k],
            device_id=self.sibling, device_id_type=pl.DeviceIdType.MESH)

    def finish(self):
        for region, i, peer in self.sent:
            self.describe(region, i, peer).wait_send()


def ring(net, reg, half, plus, minus, here, before, after, across, core):
    ids = {}

    def first():
        ids["p"] = net.put(lambda: reg(here), plus)
        ids["m"] = net.put(lambda: reg(here), minus)

    def second():
        net.got(lambda: reg(before), ids["p"])
        net.got(lambda: reg(after), ids["m"])
        ids["pp"] = net.put(lambda: half(before, 0), plus)
        ids["mm"] = net.put(lambda: half(after, 1), minus)
        core(lambda: reg(before))
        core(lambda: reg(after))

    def third():
        net.got(lambda: half(across, 0), ids["pp"])
        net.got(lambda: half(across, 1), ids["mm"])
        core(lambda: reg(across))

    return [first, second, third]


def chain(*rings):
    steps = list(rings[0])
    for following in rings[1:]:
        last = steps.pop()

        def joined(last=last, start=following[0]):
            last()
            start()

        steps.append(joined)
        steps.extend(following[1:])
    return steps


def beside(*lists):
    def step(k):
        def run():
            for steps in lists:
                steps[k]()
        return run
    return [step(k) for k in range(len(lists[0]))]


def kernel(lengths, resp, prompt, gain, wq, wk, wv, q_bias, k_bias, v_bias, wo, cos_b, sin_b, cos_a, sin_a,
           resid_out, squares,
           x_resp, x_prompt, wq_all, wkv_all, wo_one, wo_two, kv_all, kv_own, q_all, attended, acc,
           send, recv, core_send, core_recv, att_send, att_recv, local, out_sem):
    g, s, t = lax.axis_index("group"), lax.axis_index("sample"), lax.axis_index("tensor")
    z, xh, c = s // 4, lax.rem(s // 2, 2), lax.rem(s, 2)
    x = 2 * xh + g

    def wrap(v):
        return lax.rem(v + 4, 4)

    def place(zz, xx, cc, tt):
        return (lax.rem(xx, 2), zz * 4 + (xx // 2) * 2 + cc, tt)

    zm, zp, z2 = wrap(z - 1), wrap(z + 1), wrap(z + 2)
    xm, xp, x2 = wrap(x - 1), wrap(x + 1), wrap(x + 2)
    tm, tp, t2 = wrap(t - 1), wrap(t + 1), wrap(t + 2)
    at_zp, at_zm = place(zp, x, c, t), place(zm, x, c, t)
    at_xp, at_xm, at_x2 = place(z, xp, c, t), place(z, xm, c, t), place(z, x2, c, t)
    at_tp, at_tm = place(z, x, c, tp), place(z, x, c, tm)
    sibling = place(z, x, 1 - c, t)
    other = 1 - xh

    part = pl.ds(pl.multiple_of(g * 160, 160), 160)
    part_one = pl.ds(pl.multiple_of(g * 160, 160), 80)
    part_two = pl.ds(pl.multiple_of(g * 160 + 80, 80), 80)
    loads = [
        pltpu.make_async_copy(wk.at[part], wkv_all.at[c, z, xh, g, :, pl.ds(0, 128)], local.at[0]),
        pltpu.make_async_copy(wv.at[part], wkv_all.at[c, z, xh, g, :, pl.ds(128, 128)], local.at[1]),
        pltpu.make_async_copy(wq.at[part], wq_all.at[c, z, xh, g], local.at[2]),
        pltpu.make_async_copy(wo.at[part_one], wo_one.at[c, t, z, xh, g], local.at[3]),
        pltpu.make_async_copy(wo.at[part_two], wo_two.at[c, z, xh, g, t], local.at[4]),
        pltpu.make_async_copy(prompt, x_prompt, local.at[5]),
        pltpu.make_async_copy(resp, x_resp, local.at[6]),
    ]
    for load in loads:
        load.start()

    barrier = pltpu.get_barrier_semaphore()
    for peer in (at_zp, at_zm, at_xp, at_xm, at_x2, at_tp, at_tm, sibling):
        pl.semaphore_signal(barrier, inc=1, device_id=peer, device_id_type=pl.DeviceIdType.MESH)
    pl.semaphore_wait(barrier, 8)

    net = Net(send, recv, core_send, core_recv, sibling)

    def to_core(k):
        return lambda region: net.core(region, k).start()

    def rows_half(r0, count, which):
        low = (count // 2 + 15) // 16 * 16
        return pl.ds(r0, low) if which == 0 else pl.ds(r0 + low, count - low)

    def plane(reg, split_a, split_b, core):
        (ra, na, ca), (rb, nb, cb) = split_a, split_b
        da, db = pl.ds(ra, na), pl.ds(rb, nb)
        where = {"m": (xm // 2, lax.rem(xm, 2)), "p": (xp // 2, lax.rem(xp, 2)), "h": (xh, g), "2": (x2 // 2, lax.rem(x2, 2))}
        a1 = ring(net, lambda p: reg(p, xh, g, da, ca), lambda p, w: reg(p, xh, g, rows_half(ra, na, w), ca),
                  at_zp, at_zm, z, zm, zp, z2, core)
        a2 = ring(net, lambda p: reg(ALL, *where[p], da, ca), lambda p, w: reg(pl.ds(2 * w, 2), *where[p], da, ca),
                  at_xp, at_xm, "h", "m", "p", "2", core)
        b1 = ring(net, lambda p: reg(z, *where[p], db, cb), lambda p, w: reg(z, *where[p], rows_half(rb, nb, w), cb),
                  at_xp, at_xm, "h", "m", "p", "2", core)
        b2 = ring(net, lambda p: reg(p, ALL, ALL, db, cb), lambda p, w: reg(p, pl.ds(w, 1), ALL, db, cb),
                  at_zp, at_zm, z, zm, zp, z2, core)
        steps = beside(chain(a1, a2), chain(b1, b2))
        start = steps[0]

        def first():
            start()
            core(lambda: reg(z, xh, g, ALL, ALL))

        steps[0] = first
        return steps

    wkv_steps = plane(lambda zz, hh, gg, r, k: wkv_all.at[c, zz, hh, gg, r, k],
                      (0, 160, pl.ds(0, 128)), (0, 160, pl.ds(128, 128)), to_core(0))
    wq_steps = plane(lambda zz, hh, gg, r, k: wq_all.at[c, zz, hh, gg, r, k],
                     (0, 80, ALL), (80, 80, ALL), to_core(1))
    one_steps = chain(
        plane(lambda zz, hh, gg, r, k: wo_one.at[c, t, zz, hh, gg, r, k],
              (0, 80, pl.ds(0, 384)), (0, 80, pl.ds(384, 256)), to_core(2)),
        ring(net, lambda p: wo_one.at[c, p], lambda p, w: wo_one.at[c, p, pl.ds(2 * w, 2)],
             at_tp, at_tm, t, tm, tp, t2, to_core(2)))
    two_steps = chain(
        ring(net, lambda p: wo_two.at[c, z, xh, g, p],
             lambda p, w: wo_two.at[c, z, xh, g, p, rows_half(0, 80, w)],
             at_tp, at_tm, t, tm, tp, t2, lambda region: None),
        plane(lambda zz, hh, gg, r, k: wo_two.at[c, zz, hh, gg, :, r, k],
              (0, 80, pl.ds(0, 256)), (0, 80, pl.ds(256, 384)), to_core(3)))

    ka, kb = pl.ds(0, 224), pl.ds(224, 288)
    kv_core = to_core(4)
    kv_ids = {}
    kv_za = ring(net, lambda p: kv_all.at[c, p, xh, ka], lambda p, w: kv_all.at[c, p, xh, pl.ds(112 * w, 112)],
                 at_zp, at_zm, z, zm, zp, z2, kv_core)
    kv_zb = ring(net, lambda p: kv_all.at[c, p, :, kb], lambda p, w: kv_all.at[c, p, pl.ds(w, 1), kb],
                 at_zp, at_zm, z, zm, zp, z2, kv_core)

    def kv_0():
        kv_za[0]()
        kv_ids["b"] = net.put(lambda: kv_all.at[c, z, xh, kb], at_x2)
        kv_core(lambda: kv_all.at[c, z, xh])

    def kv_1():
        kv_za[1]()
        net.got(lambda: kv_all.at[c, z, other, kb], kv_ids["b"])
        kv_core(lambda: kv_all.at[c, z, other, kb])
        kv_zb[0]()

    def kv_2():
        kv_za[2]()
        kv_ids["a"] = net.put(lambda: kv_all.at[c, :, xh, ka], at_x2)
        kv_zb[1]()

    def kv_3():
        net.got(lambda: kv_all.at[c, :, other, ka], kv_ids["a"])
        kv_core(lambda: kv_all.at[c, :, other, ka])
        kv_zb[2]()

    def core_in(k, buf):
        net.core(lambda: buf.at[1 - c], k).wait_recv()

    gain_row = gain[...].astype(F32)

    def normalize(ref):
        def rows16(i, _):
            r = pl.ds(pl.multiple_of(i * 16, 16), 16)
            v = ref[r, :].astype(F32)
            scale = lax.rsqrt(jnp.mean(v * v, axis=-1, keepdims=True) + EPS)
            ref[r, :] = (v * scale * gain_row).astype(BF16)
            return 0
        lax.fori_loop(0, ROWS // 16, rows16, 0)

    def project(rows_ref, weights, width):
        acc[:, :width] = jnp.zeros((ROWS, width), F32)

        def block(i, _):
            left = rows_ref[:, pl.ds(pl.multiple_of(i * 640, 640), 640)]
            zz, hh = i // 2, lax.rem(i, 2)
            right = jnp.concatenate(
                [weights[0, zz, hh].reshape(320, width), weights[1, zz, hh].reshape(320, width)], 0)
            acc[:, :width] += jnp.dot(left, right, preferred_element_type=F32)
            return 0
        lax.fori_loop(0, 8, block, 0)

    def angles(block):
        ca, sa = cos_a[pl.ds(block, 1), :], sin_a[pl.ds(block, 1), :]
        cb, sb = cos_b[...], sin_b[...]
        lane = lax.broadcasted_iota(jnp.int32, (ROWS, HEAD), 1)
        sine = sa * cb + ca * sb
        return ca * cb - sa * sb, jnp.where(lane < HEAD // 2, -sine, sine)

    def rope(u, cosine, sine):
        return u * cosine + pltpu.roll(u, HEAD // 2, 1) * sine

    def keys_values(block):
        cosine, sine = angles(block)
        keys = rope(acc[:, 0:128] + k_bias[...].astype(F32), cosine, sine).astype(BF16)
        return keys, (acc[:, 128:256] + v_bias[...].astype(F32)).astype(BF16)

    loads[0].wait()
    loads[1].wait()
    wkv_steps[0]()
    loads[2].wait()
    loads[3].wait()
    loads[4].wait()
    two_steps[0]()
    wq_steps[0]()
    loads[5].wait()
    normalize(x_prompt)
    wkv_steps[1]()
    two_steps[1]()
    wkv_steps[2]()
    one_steps[0]()
    wq_steps[1]()
    wkv_steps[3]()
    loads[6].wait()
    normalize(x_resp)
    wkv_steps[4]()
    one_steps[1]()
    wq_steps[2]()
    core_in(0, wkv_all)
    project(x_prompt, wkv_all, 256)
    keys, values = keys_values(s)
    kv_all[c, z, xh, :, 0:128] = keys
    kv_all[c, z, xh, :, 128:256] = values
    kv_0()
    one_steps[2]()
    project(x_resp, wkv_all, 256)
    keys, values = keys_values(16)
    kv_own[:, 0:128] = keys
    kv_own[:, 128:256] = values
    wq_steps[3]()
    kv_1()
    one_steps[3]()
    kv_2()
    wq_steps[4]()
    one_steps[4]()
    core_in(1, wq_all)
    project(x_resp, wq_all, Q_COLS)
    cosine, sine = angles(16)
    for h in range(Q_HEADS):
        cols = slice(h * HEAD, (h + 1) * HEAD)
        q = rope(acc[:, cols] + q_bias[:, cols].astype(F32), cosine, sine)
        q_all[h] = (q * (math.log2(math.e) / math.sqrt(HEAD))).astype(BF16)
    reload = pltpu.make_async_copy(resp, x_resp, local.at[7])
    reload.start()
    kv_3()
    two_steps[2]()
    core_in(4, kv_all)

    length = lengths[0]

    def att_copy(h, k, region, peer):
        return pltpu.make_async_remote_copy(
            src_ref=region, dst_ref=region, send_sem=att_send.at[h, k], recv_sem=att_recv.at[h, k],
            device_id=peer, device_id_type=pl.DeviceIdType.MESH)

    def att_first(h):
        att_copy(h, 0, attended.at[t, h], at_tp).start()
        att_copy(h, 1, attended.at[t, h], at_tm).start()

    def att_second(h):
        att_copy(h, 0, attended.at[tm, h], at_tp).wait_recv()
        att_copy(h, 1, attended.at[tp, h], at_tm).wait_recv()
        att_copy(h, 2, attended.at[tm, h, pl.ds(0, 256)], at_tp).start()
        att_copy(h, 3, attended.at[tp, h, pl.ds(256, 256)], at_tm).start()

    def att_third(h):
        att_copy(h, 2, attended.at[t2, h, pl.ds(0, 256)], at_tp).wait_recv()
        att_copy(h, 3, attended.at[t2, h, pl.ds(256, 256)], at_tm).wait_recv()

    def att_sent(h):
        att_copy(h, 0, attended.at[t, h], at_tp).wait_send()
        att_copy(h, 1, attended.at[t, h], at_tm).wait_send()
        att_copy(h, 2, attended.at[tm, h, pl.ds(0, 256)], at_tp).wait_send()
        att_copy(h, 3, attended.at[tp, h, pl.ds(256, 256)], at_tm).wait_send()

    def head(h, _):
        q = q_all[h]

        def scores(j):
            k = kv_all[j // 2, pl.ds(2 * (j % 2), 2), :, :, 0:128].reshape(2048, HEAD)
            return lax.dot_general(q, k, NT, preferred_element_type=F32)

        def widened(v):
            return jnp.concatenate([v, jnp.ones_like(v)], 1)

        score = lax.dot_general(q, kv_own[:, 0:128], NT, preferred_element_type=F32)
        row = lax.broadcasted_iota(jnp.int32, (ROWS, ROWS), 0)
        col = lax.broadcasted_iota(jnp.int32, (ROWS, ROWS), 1)
        score = jnp.where(col <= row, score, -1e30)
        value = widened(kv_own[:, 128:256])
        highest = total = None
        for j in range(5):
            if j < 4:
                score_next = scores(j)
                value_next = widened(kv_all[j // 2, pl.ds(2 * (j % 2), 2), :, :, 128:256].reshape(2048, HEAD))
            top = jnp.max(score, axis=1, keepdims=True)
            fresh = top if j == 0 else jnp.maximum(highest, top)
            probs = jnp.exp2(score - fresh).astype(BF16)
            term = jnp.dot(probs, value, preferred_element_type=F32)
            total = term if j == 0 else total * jnp.exp2(highest - fresh) + term
            highest = fresh
            score, value = score_next, value_next
        live = lax.broadcasted_iota(jnp.int32, (ROWS, HEAD), 0) < length
        attended[t, h] = jnp.where(live, total[:, :HEAD] / total[:, HEAD:], 0.0).astype(BF16)
        att_first(h)

        @pl.when(h > 0)
        def _():
            att_second(h - 1)

        @pl.when(h == 0)
        def _():
            two_steps[3]()

        @pl.when(h == 1)
        def _():
            two_steps[4]()

        @pl.when(h == 2)
        def _():
            one_steps[5]()

        @pl.when(h == 3)
        def _():
            two_steps[5]()
        return 0

    lax.fori_loop(0, Q_HEADS, head, 0)
    att_second(Q_HEADS - 1)
    one_steps[6]()
    two_steps[6]()
    for h in range(Q_HEADS):
        att_third(h)
    core_in(2, wo_one)
    core_in(3, wo_two)
    reload.wait()

    squares[...] = jnp.zeros((ROWS, 128), F32)

    def out_copy(i):
        cols = pl.ds(pl.multiple_of(i * 640, 640), 640)
        return pltpu.make_async_copy(x_prompt.at[:, cols], resid_out.at[:, cols], out_sem.at[i])

    def block(i, _):
        zz, hh = i // 2, lax.rem(i, 2)
        cols = pl.ds(pl.multiple_of(i * 640, 640), 640)
        total = x_resp[:, cols].astype(F32)
        for tt in range(4):
            left = jnp.concatenate([attended[tt, h] for h in range(Q_HEADS)], 1)
            right = jnp.concatenate(
                [buf for cc in range(2) for gg in range(2)
                 for buf in (wo_one[cc, tt, zz, hh, gg], wo_two[cc, zz, hh, gg, tt])], 0)
            total = total + lax.dot_general(left, right, NT, preferred_element_type=F32)
        x_prompt[:, cols] = total.astype(BF16)
        square = total * total
        squares[...] += sum(square[:, k * 128:(k + 1) * 128] for k in range(5))
        out_copy(i).start()
        return 0

    lax.fori_loop(0, 8, block, 0)

    net.finish()
    for k, buf in enumerate((wkv_all, wq_all, wo_one, wo_two, kv_all)):
        net.core(lambda: buf.at[c], k).wait_send()
    for h in range(Q_HEADS):
        att_sent(h)
    for i in range(8):
        out_copy(i).wait()


def on_device(resp_hidden, prompt_hidden, lengths, norm_gain, wq, wk, wv, q_bias, k_bias, value_bias, wo_t, post_gain):
    resp = resp_hidden[0]
    tables = [jnp.asarray(a) for a in rope_tables()]
    vmem = pl.BlockSpec(memory_space=pltpu.VMEM)
    hbm = pl.BlockSpec(memory_space=pl.ANY)
    smem = pl.BlockSpec(memory_space=pltpu.SMEM)
    dma = pltpu.SemaphoreType.DMA
    resid, squares = pl.pallas_call(
        kernel,
        out_shape=(jax.ShapeDtypeStruct((ROWS, WIDTH), BF16), jax.ShapeDtypeStruct((ROWS, 128), F32)),
        in_specs=[smem, hbm, hbm, vmem, hbm, hbm, hbm, vmem, vmem, vmem, hbm, vmem, vmem, vmem, vmem],
        out_specs=(hbm, vmem),
        scratch_shapes=[
            pltpu.VMEM((ROWS, WIDTH), BF16),
            pltpu.VMEM((ROWS, WIDTH), BF16),
            pltpu.VMEM((2, 4, 2, 2, 160, Q_COLS), BF16),
            pltpu.VMEM((2, 4, 2, 2, 160, 256), BF16),
            pltpu.VMEM((2, 4, 4, 2, 2, 80, Q_COLS), BF16),
            pltpu.VMEM((2, 4, 2, 2, 4, 80, Q_COLS), BF16),
            pltpu.VMEM((2, 4, 2, ROWS, 256), BF16),
            pltpu.VMEM((ROWS, 256), BF16),
            pltpu.VMEM((Q_HEADS, ROWS, HEAD), BF16),
            pltpu.VMEM((4, Q_HEADS, ROWS, HEAD), BF16),
            pltpu.VMEM((ROWS, Q_COLS), F32),
            dma((90,)), dma((90,)), dma((5,)), dma((5,)), dma((Q_HEADS, 4)), dma((Q_HEADS, 4)), dma((8,)), dma((8,)),
        ],
        compiler_params=pltpu.CompilerParams(
            collective_id=0, has_side_effects=True, vmem_limit_bytes=67000000),
        cost_estimate=pl.CostEstimate(flops=31_000_000_000, bytes_accessed=30_000_000, transcendentals=22_000_000),
    )(lengths, resp, prompt_hidden, norm_gain[None], wq, wk, wv, q_bias[None], k_bias[None], value_bias[None], wo_t,
      *tables)
    meansq = jnp.sum(squares, axis=-1, keepdims=True) / WIDTH
    live = (jnp.arange(ROWS) < lengths[0])[:, None]
    mixed = resid.astype(F32) * lax.rsqrt(meansq + EPS) * post_gain.astype(F32)
    return jnp.where(live, mixed, 0.0).astype(BF16)[None]


def solution(mesh):
    placed = (
        P(("group", "sample"), None, None),
        P(("group", "sample"), None),
        P(("group", "sample")),
        P(),
        P("sample", "tensor"),
        P("sample", "tensor"),
        P("sample", "tensor"),
        P("tensor"),
        P("tensor"),
        P("tensor"),
        P("sample", "tensor"),
        P(),
    )
    return jax.shard_map(
        on_device,
        mesh=mesh,
        in_specs=placed,
        out_specs=P(("group", "sample"), None, None),
        check_vma=False,
    )
```

time: 530 us -> 175 us (0.33)
  waiting for transfers between devices: 312 us -> 0 us
  Pallas kernels: 0 us -> 161 us
  matrix products: 75.3 us -> 0 us
  other arithmetic: 84.3 us -> 9.65 us
  local copies, waits for them, and re-layouts: 42.7 us -> 2.6 us
  between operations: 14.4 us -> 0.68 us
    all_gather x6 -> x0, waiting for transfers between devices: 201 us -> none  [the longest x1 62.6 us: on_device(): lax.all_gather(wq, 'sample', axis=0, tiled=True)]
    pallas_call x0 -> x1, Pallas kernels: none -> 161 us  [on_device(): pl.pallas_call(kernel, out_shape=(jax.ShapeDtypeStruct((ROWS, WIDTH), BF1...]
    psum x1 -> x0, waiting for transfers between devices: 108 us -> none  [on_device(): lax.psum(terms.astype(jnp.bfloat16), 'tensor').astype(jnp.float32)]
    dot_general x24 -> x0, matrix products: 75.3 us -> none  [the longest x10 27.6 us: absorb(): jnp.dot(expd.astype(jnp.bfloat16), block_values, preferred_element_type=j...]
    reduce_sum x13 -> x1, other arithmetic: 56 us -> 1.1 us  [on_device(): meansq = jnp.sum(squares, axis=-1, keepdims=True) / WIDTH]
    while x22 -> x0, local copies, waits for them, and re-layouts: 33.2 us -> none
    convert_element_type x8 -> x1, other arithmetic: 12.7 us -> 0.7 us  [on_device(): mixed = resid.astype(F32) * lax.rsqrt(meansq + EPS) * post_gain.astype(F32)]
  transfers between devices with their start and end apart: 7 -> 0, of which waited for: 6 -> 0; matrix products, arithmetic and copies ran while one was open for 28% -> 0% of each run, Pallas kernels for 0% -> 0%
where the time goes in v1:
time: 175 us; the launch traced here: 174 us
  Pallas kernels  161 us (92%)
  other arithmetic  9.65 us (6%)
  local copies, waits for them, and re-layouts  2.6 us (1%)
    pallas_call x1, Pallas kernels, on_device(): pl.pallas_call(kernel, out_shape=(jax.ShapeDtypeStruct((ROWS, WIDTH), BF1...  161 us
    broadcast_in_dim x1, other arithmetic, on_device(): return jnp.where(live, mixed, 0.0).astype(BF16)[None]  7.84 us

profile of v1, /device:TPU:1, one launch (start us, length us, event | category | flops | bytes accessed | tf_op | source)
XLA Modules:
  0.0 174.3 jit_solution(7642142369396188862)
XLA Ops:
  0.7 1.3 broadcast_in_dim.32.q_bias
  1.9 1.3 broadcast_in_dim.31.gain
  3.3 0.7 convert_element_type.10
  4.0 161.4 %shard_map.154 = (bf16[512,5120]{1,0:T(8,128)(2,1)}, f32[512,128]{1,0:T(8,128)}) custom-call(s32[1]{0:T(128)} %copy.17.lengths, bf16[512,5120]{1,0:T(8,128)(2,1)} %bitcast.7, bf16[512,5120]{1,0:T(8,128)(2,1)} %prompt.1, bf16[1,5120]{1,0:T(2,128)(2,1)} %broadcast_in_dim.31.gain, bf16[320,640]{1,0:T(8,128)(2,1)} %wq.1, bf16[320,128]{1,0:T(8,128)(2,1)} %wk.1, ...), custom_call_target="tpu_custom_call" | custom-call | flops 31000000512 | bytes 30000000 | tf_op jit(solution)/shard_map/pallas_call | solution.py:457
  165.3 1.1 reduce_sum.9
  166.5 7.8 %fusion = bf16[1,512,5120]{2,1,0:T(8,128)(2,1)} fusion(bf16[512,5120]{1,0:T(8,128)(2,1)} %get-tuple-element.7, f32[5120]{0:T(1024)S(1)} %convert_element_type.10, f32[512]{0:T(512)S(1)} %add_rsqrt_fusion, pred[512]{0:T(512)(128)(4,1)S(1)} %iota_compare_fusion), kind=kLoop, calls=%fused_computation.1 | loop fusion | flops 13107200 | bytes 10508800 | tf_op jit(solution)/shard_map/broadcast_in_dim | solution.py:484
  (2 shorter events, 0.0 us)

commit v2 on v1

v2 whole, which is shorter than its diff:
```python
import math

import jax
import jax.numpy as jnp
import numpy as np
from jax import lax
from jax.experimental import pallas as pl
from jax.experimental.pallas import tpu as pltpu
from jax.sharding import PartitionSpec as P

HEAD = 128
EPS = 1e-06
THETA = 1000000.0
WIDTH = 5120
ROWS = 512
Q_HEADS = 5
Q_COLS = Q_HEADS * HEAD
F32 = jnp.float32
BF16 = jnp.bfloat16
NT = (((1,), (1,)), ((), ()))
ALL = slice(None)
ONE = 64
TWO = 160 - ONE


def rope_tables():
    half = np.arange(HEAD // 2, dtype=np.float64)
    inverse = THETA ** (-2.0 * half / HEAD)

    def pair(positions):
        angle = positions[:, None] * inverse[None, :]
        cosine, sine = np.cos(angle), np.sin(angle)
        both = np.concatenate([cosine, cosine], 1), np.concatenate([sine, sine], 1)
        return both[0].astype(np.float32), both[1].astype(np.float32)

    return pair(np.arange(ROWS, dtype=np.float64)) + pair(np.arange(24, dtype=np.float64) * ROWS)


class Net:
    def __init__(self, send, recv, core_send, core_recv, sibling, c):
        self.send, self.recv, self.core_send, self.core_recv = send, recv, core_send, core_recv
        self.sibling = sibling
        self.c = self.who = c
        self.count = 0
        self.sent = []
        self.shared = []

    def describe(self, region, i, peer):
        ref = region()
        return pltpu.make_async_remote_copy(
            src_ref=ref, dst_ref=ref, send_sem=self.send.at[i], recv_sem=self.recv.at[i],
            device_id=peer, device_id_type=pl.DeviceIdType.MESH)

    def put(self, region, peer):
        i = self.count
        self.count += 1
        self.describe(region, i, peer).start()
        self.sent.append((region, i, peer))
        return i

    def got(self, region, i):
        self.describe(region, i, self.sibling).wait_recv()

    def describe_core(self, region, i):
        ref = region()
        return pltpu.make_async_remote_copy(
            src_ref=ref, dst_ref=ref, send_sem=self.core_send.at[i], recv_sem=self.core_recv.at[i],
            device_id=self.sibling, device_id_type=pl.DeviceIdType.MESH)

    def core(self, region, group):
        i = len(self.shared)
        self.describe_core(region, i).start()
        self.shared.append((region, group))

    def core_in(self, group):
        self.who = 1 - self.c
        for i, (region, belongs) in enumerate(self.shared):
            if belongs == group:
                self.describe_core(region, i).wait_recv()
        self.who = self.c

    def finish(self):
        for region, i, peer in self.sent:
            self.describe(region, i, peer).wait_send()
        for i, (region, _) in enumerate(self.shared):
            self.describe_core(region, i).wait_send()


def ring(net, reg, half, plus, minus, here, before, after, across, core, core_last=None):
    ids = {}

    def first():
        ids["p"] = net.put(lambda: reg(here), plus)
        ids["m"] = net.put(lambda: reg(here), minus)

    def second():
        net.got(lambda: reg(before), ids["p"])
        net.got(lambda: reg(after), ids["m"])
        ids["pp"] = net.put(lambda: half(before, 0), plus)
        ids["mm"] = net.put(lambda: half(after, 1), minus)
        core(lambda: reg(before))
        core(lambda: reg(after))

    def third():
        net.got(lambda: half(across, 0), ids["pp"])
        net.got(lambda: half(across, 1), ids["mm"])
        (core_last or core)(lambda: reg(across))

    return [first, second, third]


def direct(net, reg, plus, minus, far, here, before, after, across, core):
    ids = {}

    def first():
        ids["p"] = net.put(lambda: reg(here), plus)
        ids["m"] = net.put(lambda: reg(here), minus)
        ids["f"] = net.put(lambda: reg(here), far)

    def second():
        net.got(lambda: reg(before), ids["p"])
        net.got(lambda: reg(after), ids["m"])
        core(lambda: reg(before))
        core(lambda: reg(after))
        net.got(lambda: reg(across), ids["f"])
        core(lambda: reg(across))

    return [first, second]


def chain(*rings):
    steps = list(rings[0])
    for following in rings[1:]:
        last = steps.pop()

        def joined(last=last, start=following[0]):
            last()
            start()

        steps.append(joined)
        steps.extend(following[1:])
    return steps


def beside(*lists):
    def step(k):
        def run():
            for steps in lists:
                steps[k]()
        return run
    return [step(k) for k in range(len(lists[0]))]


def kernel(lengths, resp, prompt, gain, wq, wk, wv, q_bias, k_bias, v_bias, wo, cos_b, sin_b, cos_a, sin_a,
           resid_out,
           x_resp, x_prompt, wq_all, wkv_all, wo_one, wo_two, kv_all, kv_own, q_all, attended, acc,
           send, recv, core_send, core_recv, att_send, att_recv, local, out_sem):
    g, s, t = lax.axis_index("group"), lax.axis_index("sample"), lax.axis_index("tensor")
    z, xh, c = s // 4, lax.rem(s // 2, 2), lax.rem(s, 2)
    x = 2 * xh + g

    def wrap(v):
        return lax.rem(v + 4, 4)

    def place(zz, xx, cc, tt):
        return (lax.rem(xx, 2), zz * 4 + (xx // 2) * 2 + cc, tt)

    zm, zp, z2 = wrap(z - 1), wrap(z + 1), wrap(z + 2)
    xm, xp, x2 = wrap(x - 1), wrap(x + 1), wrap(x + 2)
    tm, tp, t2 = wrap(t - 1), wrap(t + 1), wrap(t + 2)
    at_zp, at_zm = place(zp, x, c, t), place(zm, x, c, t)
    at_xp, at_xm, at_x2 = place(z, xp, c, t), place(z, xm, c, t), place(z, x2, c, t)
    at_z2, at_t2 = place(z2, x, c, t), place(z, x, c, t2)
    at_tp, at_tm = place(z, x, c, tp), place(z, x, c, tm)
    sibling = place(z, x, 1 - c, t)
    other = 1 - xh

    part = pl.ds(pl.multiple_of(g * 160, 160), 160)
    part_one = pl.ds(pl.multiple_of(g * 160, 160), ONE)
    part_two = pl.ds(pl.multiple_of(g * 160 + ONE, 16), TWO)
    loads = [
        pltpu.make_async_copy(wk.at[part], wkv_all.at[c, z, xh, g, :, pl.ds(0, 128)], local.at[0]),
        pltpu.make_async_copy(wv.at[part], wkv_all.at[c, z, xh, g, :, pl.ds(128, 128)], local.at[1]),
        pltpu.make_async_copy(wq.at[part], wq_all.at[c, z, xh, g], local.at[2]),
        pltpu.make_async_copy(wo.at[part_one], wo_one.at[c, t, z, xh, g], local.at[3]),
        pltpu.make_async_copy(wo.at[part_two], wo_two.at[c, z, xh, g, t], local.at[4]),
        pltpu.make_async_copy(prompt, x_prompt, local.at[5]),
        pltpu.make_async_copy(resp, x_resp, local.at[6]),
    ]
    for load in loads:
        load.start()

    barrier = pltpu.get_barrier_semaphore()
    for peer in (at_zp, at_zm, at_z2, at_t2, at_xp, at_xm, at_x2, at_tp, at_tm, sibling):
        pl.semaphore_signal(barrier, inc=1, device_id=peer, device_id_type=pl.DeviceIdType.MESH)
    pl.semaphore_wait(barrier, 10)

    net = Net(send, recv, core_send, core_recv, sibling, c)

    def to_core(k):
        return lambda region: net.core(region, k)

    def rows_half(r0, count, which):
        low = (count // 2 + 15) // 16 * 16
        return pl.ds(r0, low) if which == 0 else pl.ds(r0 + low, count - low)

    def plane(reg, split_a, split_b, core, core_last=None, straight=(False, False)):
        (ra, na, ca), (rb, nb, cb) = split_a, split_b
        da, db = pl.ds(ra, na), pl.ds(rb, nb)
        where = {"m": (xm // 2, lax.rem(xm, 2)), "p": (xp // 2, lax.rem(xp, 2)), "h": (xh, g), "2": (x2 // 2, lax.rem(x2, 2))}

        def gather(stage, whole, half, axis):
            plus, minus, far, places = (at_zp, at_zm, at_z2, (z, zm, zp, z2)) if axis == "z" else (
                at_xp, at_xm, at_x2, ("h", "m", "p", "2"))
            if straight[stage]:
                return direct(net, whole, plus, minus, far, *places, core)
            return ring(net, whole, half, plus, minus, *places, core, core_last if stage else None)

        a1 = gather(0, lambda p: reg(p, xh, g, da, ca), lambda p, w: reg(p, xh, g, rows_half(ra, na, w), ca), "z")
        a2 = gather(1, lambda p: reg(ALL, *where[p], da, ca), lambda p, w: reg(pl.ds(2 * w, 2), *where[p], da, ca), "x")
        b1 = gather(0, lambda p: reg(z, *where[p], db, cb), lambda p, w: reg(z, *where[p], rows_half(rb, nb, w), cb), "x")
        b2 = gather(1, lambda p: reg(p, ALL, ALL, db, cb), lambda p, w: reg(p, pl.ds(w, 1), ALL, db, cb), "z")
        steps = beside(chain(a1, a2), chain(b1, b2))
        start = steps[0]

        def first():
            start()
            core(lambda: reg(z, xh, g, ALL, ALL))

        steps[0] = first
        return steps

    wkv_steps = plane(lambda zz, hh, gg, r, k: wkv_all.at[net.who, zz, hh, gg, r, k],
                      (0, 160, pl.ds(0, 128)), (0, 160, pl.ds(128, 128)), to_core(0))
    wq_steps = plane(lambda zz, hh, gg, r, k: wq_all.at[net.who, zz, hh, gg, r, k],
                     (0, 80, ALL), (80, 80, ALL), to_core(1))
    one_steps = chain(
        plane(lambda zz, hh, gg, r, k: wo_one.at[net.who, t, zz, hh, gg, r, k],
              (0, ONE, pl.ds(0, 384)), (0, ONE, pl.ds(384, 256)), to_core(2)),
        ring(net, lambda p: wo_one.at[net.who, p], lambda p, w: wo_one.at[net.who, p, pl.ds(2 * w, 2)],
             at_tp, at_tm, t, tm, tp, t2, to_core(2)))
    two_steps = chain(
        ring(net, lambda p: wo_two.at[net.who, z, xh, g, p],
             lambda p, w: wo_two.at[net.who, z, xh, g, p, rows_half(0, TWO, w)],
             at_tp, at_tm, t, tm, tp, t2, lambda region: None),
        plane(lambda zz, hh, gg, r, k: wo_two.at[net.who, zz, hh, gg, :, r, k],
              (0, TWO, pl.ds(0, 256)), (0, TWO, pl.ds(256, 384)), to_core(3), to_core(5)))

    ka, kb = pl.ds(0, 224), pl.ds(224, 288)
    kv_core = to_core(4)
    kv_ids = {}
    kv_za = ring(net, lambda p: kv_all.at[net.who, p, xh, ka], lambda p, w: kv_all.at[net.who, p, xh, pl.ds(112 * w, 112)],
                 at_zp, at_zm, z, zm, zp, z2, kv_core)
    kv_zb = ring(net, lambda p: kv_all.at[net.who, p, :, kb], lambda p, w: kv_all.at[net.who, p, pl.ds(w, 1), kb],
                 at_zp, at_zm, z, zm, zp, z2, kv_core)

    def kv_0():
        kv_za[0]()
        kv_ids["b"] = net.put(lambda: kv_all.at[net.who, z, xh, kb], at_x2)
        kv_core(lambda: kv_all.at[net.who, z, xh])

    def kv_1():
        kv_za[1]()
        net.got(lambda: kv_all.at[net.who, z, other, kb], kv_ids["b"])
        kv_core(lambda: kv_all.at[net.who, z, other, kb])
        kv_zb[0]()

    def kv_2():
        kv_za[2]()
        kv_ids["a"] = net.put(lambda: kv_all.at[net.who, :, xh, ka], at_x2)
        kv_zb[1]()

    def kv_3():
        net.got(lambda: kv_all.at[net.who, :, other, ka], kv_ids["a"])
        kv_core(lambda: kv_all.at[net.who, :, other, ka])
        kv_zb[2]()

    gain_row = gain[...].astype(F32).reshape(1, WIDTH)
    q_row = q_bias[...].astype(F32).reshape(1, Q_COLS)
    k_row = k_bias[...].astype(F32).reshape(1, HEAD)
    v_row = v_bias[...].astype(F32).reshape(1, HEAD)

    def normalize(ref, first, count):
        def rows32(i, _):
            r = pl.ds(pl.multiple_of(first + i * 32, 32), 32)
            v = ref[r, :].astype(F32)
            scale = lax.rsqrt(jnp.mean(v * v, axis=-1, keepdims=True) + EPS)
            ref[r, :] = (v * scale * gain_row).astype(BF16)
            return 0
        lax.fori_loop(0, count // 32, rows32, 0)

    def project(rows_ref, weights, width):
        acc[:, :width] = jnp.zeros((ROWS, width), F32)

        def block(zz, _):
            left = rows_ref[:, pl.ds(pl.multiple_of(zz * 1280, 1280), 1280)]
            right = jnp.concatenate(
                [weights[cc, zz, hh].reshape(320, width) for hh in range(2) for cc in range(2)], 0)
            acc[:, :width] += jnp.dot(left, right, preferred_element_type=F32)
            return 0
        lax.fori_loop(0, 4, block, 0)

    def angles(block):
        ca, sa = cos_a[pl.ds(block, 1), :], sin_a[pl.ds(block, 1), :]
        cb, sb = cos_b[...], sin_b[...]
        lane = lax.broadcasted_iota(jnp.int32, (ROWS, HEAD), 1)
        sine = sa * cb + ca * sb
        return ca * cb - sa * sb, jnp.where(lane < HEAD // 2, -sine, sine)

    def rope(u, cosine, sine):
        return u * cosine + pltpu.roll(u, HEAD // 2, 1) * sine

    def keys_values(block):
        cosine, sine = angles(block)
        keys = rope(acc[:, 0:128] + k_row, cosine, sine).astype(BF16)
        return keys, (acc[:, 128:256] + v_row).astype(BF16)

    loads[3].wait()
    one_steps[0]()
    loads[4].wait()
    two_steps[0]()
    loads[2].wait()
    wq_steps[0]()
    loads[0].wait()
    loads[1].wait()
    wkv_steps[0]()
    one_steps[1]()
    wq_steps[1]()
    wkv_steps[1]()
    one_steps[2]()
    two_steps[1]()
    loads[5].wait()
    normalize(x_prompt, 0, 256)
    wkv_steps[2]()
    normalize(x_prompt, 256, 256)
    one_steps[3]()
    wkv_steps[3]()
    wq_steps[2]()
    loads[6].wait()
    normalize(x_resp, 0, 256)
    one_steps[4]()
    normalize(x_resp, 256, 256)
    wkv_steps[4]()
    net.core_in(0)
    project(x_prompt, wkv_all, 256)
    keys, values = keys_values(s)
    kv_all[c, z, xh, :, 0:128] = keys
    kv_all[c, z, xh, :, 128:256] = values
    kv_0()
    two_steps[2]()
    kv_1()
    wq_steps[3]()
    two_steps[3]()
    project(x_resp, wkv_all, 256)
    keys, values = keys_values(16)
    kv_own[:, 0:128] = keys
    kv_own[:, 128:256] = values
    kv_2()
    wq_steps[4]()
    one_steps[5]()
    two_steps[4]()
    net.core_in(1)
    project(x_resp, wq_all, Q_COLS)
    cosine, sine = angles(16)
    for h in range(Q_HEADS):
        cols = slice(h * HEAD, (h + 1) * HEAD)
        q = rope(acc[:, cols] + q_row[:, cols], cosine, sine)
        q_all[h] = (q * (math.log2(math.e) / math.sqrt(HEAD))).astype(BF16)
    reload = pltpu.make_async_copy(resp, x_resp, local.at[7])
    reload.start()
    kv_3()
    net.core_in(4)

    length = lengths[0]

    def att_copy(h, k, region, peer):
        return pltpu.make_async_remote_copy(
            src_ref=region, dst_ref=region, send_sem=att_send.at[h, k], recv_sem=att_recv.at[h, k],
            device_id=peer, device_id_type=pl.DeviceIdType.MESH)

    def att_first(h):
        att_copy(h, 0, attended.at[t, h], at_tp).start()
        att_copy(h, 1, attended.at[t, h], at_tm).start()

    def att_second(h):
        att_copy(h, 0, attended.at[tm, h], at_tp).wait_recv()
        att_copy(h, 1, attended.at[tp, h], at_tm).wait_recv()
        att_copy(h, 2, attended.at[tm, h, pl.ds(0, 256)], at_tp).start()
        att_copy(h, 3, attended.at[tp, h, pl.ds(256, 256)], at_tm).start()

    def att_third(h):
        att_copy(h, 2, attended.at[t2, h, pl.ds(0, 256)], at_tp).wait_recv()
        att_copy(h, 3, attended.at[t2, h, pl.ds(256, 256)], at_tm).wait_recv()

    def att_sent(h):
        att_copy(h, 0, attended.at[t, h], at_tp).wait_send()
        att_copy(h, 1, attended.at[t, h], at_tm).wait_send()
        att_copy(h, 2, attended.at[tm, h, pl.ds(0, 256)], at_tp).wait_send()
        att_copy(h, 3, attended.at[tp, h, pl.ds(256, 256)], at_tm).wait_send()

    def head(h, _):
        q = q_all[h]

        def scores(j):
            k = kv_all[j // 2, pl.ds(2 * (j % 2), 2), :, :, 0:128].reshape(2048, HEAD)
            return lax.dot_general(q, k, NT, preferred_element_type=F32)

        def widened(v):
            return jnp.concatenate([v, jnp.ones_like(v)], 1)

        score = lax.dot_general(q, kv_own[:, 0:128], NT, preferred_element_type=F32)
        row = lax.broadcasted_iota(jnp.int32, (ROWS, ROWS), 0)
        col = lax.broadcasted_iota(jnp.int32, (ROWS, ROWS), 1)
        score = jnp.where(col <= row, score, -1e30)
        value = widened(kv_own[:, 128:256])
        highest = total = None
        for j in range(5):
            if j < 4:
                score_next = scores(j)
                value_next = widened(kv_all[j // 2, pl.ds(2 * (j % 2), 2), :, :, 128:256].reshape(2048, HEAD))
            top = jnp.max(score, axis=1, keepdims=True)
            fresh = top if j == 0 else jnp.maximum(highest, top)
            probs = jnp.exp2(score - fresh).astype(BF16)
            term = jnp.dot(probs, value, preferred_element_type=F32)
            total = term if j == 0 else total * jnp.exp2(highest - fresh) + term
            highest = fresh
            score, value = score_next, value_next
        live = lax.broadcasted_iota(jnp.int32, (ROWS, HEAD), 0) < length
        attended[t, h] = jnp.where(live, total[:, :HEAD] / total[:, HEAD:], 0.0).astype(BF16)
        att_first(h)

        @pl.when(h > 0)
        def _():
            att_second(h - 1)

        @pl.when(h == 3)
        def _():
            two_steps[5]()
            one_steps[6]()

        @pl.when(h == 4)
        def _():
            net.core_in(2)
            net.core_in(3)
        return 0

    lax.fori_loop(0, Q_HEADS, head, 0)
    att_second(Q_HEADS - 1)
    reload.wait()
    for h in range(Q_HEADS):
        att_third(h)
    two_steps[6]()
    net.core_in(5)

    def out_copy(zz):
        cols = pl.ds(pl.multiple_of(zz * 1280, 1280), 1280)
        return pltpu.make_async_copy(x_prompt.at[:, cols], resid_out.at[:, cols], out_sem.at[zz])

    def block(zz, _):
        cols = pl.ds(pl.multiple_of(zz * 1280, 1280), 1280)
        left = jnp.concatenate([attended[tt, h] for tt in range(4) for h in range(Q_HEADS)], 1)
        right = jnp.concatenate(
            [jnp.concatenate(
                [buf for hh in range(2) for cc in range(2) for gg in range(2)
                 for buf in (wo_one[cc, tt, zz, hh, gg], wo_two[cc, zz, hh, gg, tt])], 0)
             for tt in range(4)], 1)
        branch = lax.dot_general(left, right, NT, preferred_element_type=F32)
        x_prompt[:, cols] = (x_resp[:, cols].astype(F32) + branch).astype(BF16)
        out_copy(zz).start()
        return 0

    lax.fori_loop(0, 4, block, 0)

    net.finish()
    for h in range(Q_HEADS):
        att_sent(h)
    for zz in range(4):
        out_copy(zz).wait()


def finish_kernel(lengths, resid, gain, mixed):
    rows = resid.shape[0]
    v = resid[...].astype(F32)
    scale = lax.rsqrt(jnp.mean(v * v, axis=-1, keepdims=True) + EPS)
    slot = pl.program_id(0) * rows + lax.broadcasted_iota(jnp.int32, (rows, 1), 0)
    out = v * scale * gain[...].astype(F32).reshape(1, WIDTH)
    mixed[...] = jnp.where(slot < lengths[0], out, 0.0).astype(BF16)


def on_device(resp_hidden, prompt_hidden, lengths, norm_gain, wq, wk, wv, q_bias, k_bias, value_bias, wo_t, post_gain):
    resp = resp_hidden[0]
    tables = [jnp.asarray(a) for a in rope_tables()]
    vmem = pl.BlockSpec(memory_space=pltpu.VMEM)
    hbm = pl.BlockSpec(memory_space=pl.ANY)
    smem = pl.BlockSpec(memory_space=pltpu.SMEM)
    dma = pltpu.SemaphoreType.DMA
    resid = pl.pallas_call(
        kernel,
        out_shape=jax.ShapeDtypeStruct((ROWS, WIDTH), BF16),
        in_specs=[smem, hbm, hbm, vmem, hbm, hbm, hbm, vmem, vmem, vmem, hbm, vmem, vmem, vmem, vmem],
        out_specs=hbm,
        scratch_shapes=[
            pltpu.VMEM((ROWS, WIDTH), BF16),
            pltpu.VMEM((ROWS, WIDTH), BF16),
            pltpu.VMEM((2, 4, 2, 2, 160, Q_COLS), BF16),
            pltpu.VMEM((2, 4, 2, 2, 160, 256), BF16),
            pltpu.VMEM((2, 4, 4, 2, 2, ONE, Q_COLS), BF16),
            pltpu.VMEM((2, 4, 2, 2, 4, TWO, Q_COLS), BF16),
            pltpu.VMEM((2, 4, 2, ROWS, 256), BF16),
            pltpu.VMEM((ROWS, 256), BF16),
            pltpu.VMEM((Q_HEADS, ROWS, HEAD), BF16),
            pltpu.VMEM((4, Q_HEADS, ROWS, HEAD), BF16),
            pltpu.VMEM((ROWS, Q_COLS), F32),
            dma((90,)), dma((90,)), dma((70,)), dma((70,)), dma((Q_HEADS, 4)), dma((Q_HEADS, 4)), dma((8,)), dma((8,)),
        ],
        compiler_params=pltpu.CompilerParams(
            collective_id=0, has_side_effects=True, vmem_limit_bytes=67000000),
        cost_estimate=pl.CostEstimate(flops=31_000_000_000, bytes_accessed=30_000_000, transcendentals=22_000_000),
    )(lengths, resp, prompt_hidden, norm_gain, wq, wk, wv, q_bias, k_bias, value_bias, wo_t,
      *tables)
    block = pl.BlockSpec((64, WIDTH), lambda i: (i, 0))
    mixed = pl.pallas_call(
        finish_kernel,
        out_shape=jax.ShapeDtypeStruct((ROWS, WIDTH), BF16),
        grid=(ROWS // 64,),
        in_specs=[smem, block, vmem],
        out_specs=block,
    )(lengths, resid, post_gain)
    return mixed[None]


def solution(mesh):
    placed = (
        P(("group", "sample"), None, None),
        P(("group", "sample"), None),
        P(("group", "sample")),
        P(),
        P("sample", "tensor"),
        P("sample", "tensor"),
        P("sample", "tensor"),
        P("tensor"),
        P("tensor"),
        P("tensor"),
        P("sample", "tensor"),
        P(),
    )
    return jax.shard_map(
        on_device,
        mesh=mesh,
        in_specs=placed,
        out_specs=P(("group", "sample"), None, None),
        check_vma=False,
    )
```

time: 175 us -> 136 us (0.78)
  Pallas kernels: 161 us -> 134 us
  other arithmetic: 9.65 us -> 0 us
  local copies, waits for them, and re-layouts: 2.6 us -> 0 us
    pallas_call x1 -> x2, Pallas kernels: 161 us -> 134 us  [the longest x1 126 us: on_device(): pl.pallas_call(kernel, out_shape=jax.ShapeDtypeStruct((ROWS, WIDTH), BF16...]
    broadcast_in_dim x1 -> x0, other arithmetic: 7.84 us -> none  [on_device(): return jnp.where(live, mixed, 0.0).astype(BF16)[None]]
    broadcast_in_dim x2 -> x0, local copies, waits for them, and re-layouts: 2.6 us -> none  [the longest x1 1.32 us: on_device(): norm_gain[None]]
where the time goes in v2:
time: 136 us; the launch traced here: 135 us
  Pallas kernels  134 us (99%)
    pallas_call x1, Pallas kernels, on_device(): pl.pallas_call(kernel, out_shape=jax.ShapeDtypeStruct((ROWS, WIDTH), BF16...  126 us
    pallas_call x1, Pallas kernels, on_device(): pl.pallas_call(finish_kernel, out_shape=jax.ShapeDtypeStruct((ROWS, WIDTH...  8.3 us

profile of v2, /device:TPU:1, one launch (start us, length us, event | category | flops | bytes accessed | tf_op | source)
XLA Modules:
  0.0 135.1 jit_solution(2001811893762357884)
XLA Ops:
  0.7 126.2 %shard_map.154.resid = bf16[512,5120]{1,0:T(8,128)(2,1)} custom-call(s32[1]{0:T(128)S(6)} %copy.17.lengths, bf16[512,5120]{1,0:T(8,128)(2,1)} %bitcast.2, bf16[512,5120]{1,0:T(8,128)(2,1)} %prompt.1, bf16[5120]{0:T(1024)(128)(2,1)} %gain.2, bf16[320,640]{1,0:T(8,128)(2,1)} %wq.1, bf16[320,128]{1,0:T(8,128)(2,1)} %wk.1, bf16[320,128]{1,0:T(8,128)(2,1)} %wv.1, ...), custom_call_target="tpu_custom_call" | custom-call | flops 31000000512 | bytes 30000000 | tf_op jit(solution)/shard_map/pallas_call | solution.py:497
  126.8 8.3 %shard_map.155 = bf16[512,5120]{1,0:T(8,128)(2,1)} custom-call(s32[1]{0:T(128)S(6)} %copy.17.lengths, bf16[512,5120]{1,0:T(8,128)(2,1)} %shard_map.154.resid, bf16[5120]{0:T(1024)(128)(2,1)} %gain.3), custom_call_target="tpu_custom_call" | custom-call | tf_op jit(solution)/shard_map/pallas_call | solution.py:522

commit v3 on v2

--- a/solution.py
+++ b/solution.py
@@ -19,8 +19,7 @@
 BF16 = jnp.bfloat16
 NT = (((1,), (1,)), ((), ()))
 ALL = slice(None)
-ONE = 64
-TWO = 160 - ONE
+ONE, MID, TWO = 32, 48, 80
 
 
 def rope_tables():
@@ -153,7 +152,7 @@
 
 def kernel(lengths, resp, prompt, gain, wq, wk, wv, q_bias, k_bias, v_bias, wo, cos_b, sin_b, cos_a, sin_a,
            resid_out,
-           x_resp, x_prompt, wq_all, wkv_all, wo_one, wo_two, kv_all, kv_own, q_all, attended, acc,
+           x_resp, x_prompt, wq_all, wkv_all, wo_one, wo_mid, wo_two, kv_all, kv_own, q_all, attended, acc,
            send, recv, core_send, core_recv, att_send, att_recv, local, out_sem):
     g, s, t = lax.axis_index("group"), lax.axis_index("sample"), lax.axis_index("tensor")
     z, xh, c = s // 4, lax.rem(s // 2, 2), lax.rem(s, 2)
@@ -177,7 +176,8 @@
 
     part = pl.ds(pl.multiple_of(g * 160, 160), 160)
     part_one = pl.ds(pl.multiple_of(g * 160, 160), ONE)
-    part_two = pl.ds(pl.multiple_of(g * 160 + ONE, 16), TWO)
+    part_mid = pl.ds(pl.multiple_of(g * 160 + ONE, 16), MID)
+    part_two = pl.ds(pl.multiple_of(g * 160 + ONE + MID, 16), TWO)
     loads = [
         pltpu.make_async_copy(wk.at[part], wkv_all.at[c, z, xh, g, :, pl.ds(0, 128)], local.at[0]),
         pltpu.make_async_copy(wv.at[part], wkv_all.at[c, z, xh, g, :, pl.ds(128, 128)], local.at[1]),
@@ -186,6 +186,7 @@
         pltpu.make_async_copy(wo.at[part_two], wo_two.at[c, z, xh, g, t], local.at[4]),
         pltpu.make_async_copy(prompt, x_prompt, local.at[5]),
         pltpu.make_async_copy(resp, x_resp, local.at[6]),
+        pltpu.make_async_copy(wo.at[part_mid], wo_mid.at[c, t, z, xh, g], local.at[8]),
     ]
     for load in loads:
         load.start()
@@ -201,8 +202,13 @@
         return lambda region: net.core(region, k)
 
     def rows_half(r0, count, which):
-        low = (count // 2 + 15) // 16 * 16
+        low = count // 2 if count <= 4 else (count // 2 + 15) // 16 * 16
         return pl.ds(r0, low) if which == 0 else pl.ds(r0 + low, count - low)
+
+    def halved(r0, count, cols, which):
+        if count == 16:
+            return pl.ds(r0, 16), pl.ds(0, 384) if which == 0 else pl.ds(384, 256)
+        return rows_half(r0, count, which), cols
 
     def plane(reg, split_a, split_b, core, core_last=None, straight=(False, False)):
         (ra, na, ca), (rb, nb, cb) = split_a, split_b
@@ -216,9 +222,9 @@
                 return direct(net, whole, plus, minus, far, *places, core)
             return ring(net, whole, half, plus, minus, *places, core, core_last if stage else None)
 
-        a1 = gather(0, lambda p: reg(p, xh, g, da, ca), lambda p, w: reg(p, xh, g, rows_half(ra, na, w), ca), "z")
+        a1 = gather(0, lambda p: reg(p, xh, g, da, ca), lambda p, w: reg(p, xh, g, *halved(ra, na, ca, w)), "z")
         a2 = gather(1, lambda p: reg(ALL, *where[p], da, ca), lambda p, w: reg(pl.ds(2 * w, 2), *where[p], da, ca), "x")
-        b1 = gather(0, lambda p: reg(z, *where[p], db, cb), lambda p, w: reg(z, *where[p], rows_half(rb, nb, w), cb), "x")
+        b1 = gather(0, lambda p: reg(z, *where[p], db, cb), lambda p, w: reg(z, *where[p], *halved(rb, nb, cb, w)), "x")
         b2 = gather(1, lambda p: reg(p, ALL, ALL, db, cb), lambda p, w: reg(p, pl.ds(w, 1), ALL, db, cb), "z")
         steps = beside(chain(a1, a2), chain(b1, b2))
         start = steps[0]
@@ -231,25 +237,28 @@
         return steps
 
     wkv_steps = plane(lambda zz, hh, gg, r, k: wkv_all.at[net.who, zz, hh, gg, r, k],
-                      (0, 160, pl.ds(0, 128)), (0, 160, pl.ds(128, 128)), to_core(0))
+                      (0, 160, pl.ds(0, 128)), (0, 160, pl.ds(128, 128)), to_core(0), straight=(True, False))
     wq_steps = plane(lambda zz, hh, gg, r, k: wq_all.at[net.who, zz, hh, gg, r, k],
                      (0, 80, ALL), (80, 80, ALL), to_core(1))
-    one_steps = chain(
-        plane(lambda zz, hh, gg, r, k: wo_one.at[net.who, t, zz, hh, gg, r, k],
-              (0, ONE, pl.ds(0, 384)), (0, ONE, pl.ds(384, 256)), to_core(2)),
-        ring(net, lambda p: wo_one.at[net.who, p], lambda p, w: wo_one.at[net.who, p, pl.ds(2 * w, 2)],
-             at_tp, at_tm, t, tm, tp, t2, to_core(2)))
+    def plane_then_y(buf, split_a, split_b, k, k_last):
+        return chain(
+            plane(lambda zz, hh, gg, r, cols: buf.at[net.who, t, zz, hh, gg, r, cols], split_a, split_b, to_core(k)),
+            ring(net, lambda p: buf.at[net.who, p], lambda p, w: buf.at[net.who, p, pl.ds(2 * w, 2)],
+                 at_tp, at_tm, t, tm, tp, t2, to_core(k), to_core(k_last)))
+
+    one_steps = plane_then_y(wo_one, (0, 16, ALL), (16, 16, ALL), 2, 6)
+    mid_steps = plane_then_y(wo_mid, (0, MID, pl.ds(0, 256)), (0, MID, pl.ds(256, 384)), 7, 8)
     two_steps = chain(
         ring(net, lambda p: wo_two.at[net.who, z, xh, g, p],
              lambda p, w: wo_two.at[net.who, z, xh, g, p, rows_half(0, TWO, w)],
              at_tp, at_tm, t, tm, tp, t2, lambda region: None),
-        plane(lambda zz, hh, gg, r, k: wo_two.at[net.who, zz, hh, gg, :, r, k],
-              (0, TWO, pl.ds(0, 256)), (0, TWO, pl.ds(256, 384)), to_core(3), to_core(5)))
-
-    ka, kb = pl.ds(0, 224), pl.ds(224, 288)
+        plane(lambda zz, hh, gg, r, k: wo_two.at[net.who, zz, hh, gg, r],
+              (0, 2, ALL), (2, 2, ALL), to_core(3), to_core(5)))
+
+    ka, kb = pl.ds(0, 192), pl.ds(192, 320)
     kv_core = to_core(4)
     kv_ids = {}
-    kv_za = ring(net, lambda p: kv_all.at[net.who, p, xh, ka], lambda p, w: kv_all.at[net.who, p, xh, pl.ds(112 * w, 112)],
+    kv_za = ring(net, lambda p: kv_all.at[net.who, p, xh, ka], lambda p, w: kv_all.at[net.who, p, xh, pl.ds(96 * w, 96)],
                  at_zp, at_zm, z, zm, zp, z2, kv_core)
     kv_zb = ring(net, lambda p: kv_all.at[net.who, p, :, kb], lambda p, w: kv_all.at[net.who, p, pl.ds(w, 1), kb],
                  at_zp, at_zm, z, zm, zp, z2, kv_core)
@@ -289,8 +298,9 @@
             return 0
         lax.fori_loop(0, count // 32, rows32, 0)
 
-    def project(rows_ref, weights, width):
-        acc[:, :width] = jnp.zeros((ROWS, width), F32)
+    def project(rows_ref, weights, width, first=0, last=4):
+        if first == 0:
+            acc[:, :width] = jnp.zeros((ROWS, width), F32)
 
         def block(zz, _):
             left = rows_ref[:, pl.ds(pl.multiple_of(zz * 1280, 1280), 1280)]
@@ -298,7 +308,7 @@
                 [weights[cc, zz, hh].reshape(320, width) for hh in range(2) for cc in range(2)], 0)
             acc[:, :width] += jnp.dot(left, right, preferred_element_type=F32)
             return 0
-        lax.fori_loop(0, 4, block, 0)
+        lax.fori_loop(first, last, block, 0)
 
     def angles(block):
         ca, sa = cos_a[pl.ds(block, 1), :], sin_a[pl.ds(block, 1), :]
@@ -317,30 +327,35 @@
 
     loads[3].wait()
     one_steps[0]()
+    loads[7].wait()
+    mid_steps[0]()
+    loads[0].wait()
+    loads[1].wait()
+    wkv_steps[0]()
+    one_steps[1]()
     loads[4].wait()
     two_steps[0]()
     loads[2].wait()
     wq_steps[0]()
-    loads[0].wait()
-    loads[1].wait()
-    wkv_steps[0]()
-    one_steps[1]()
-    wq_steps[1]()
+    one_steps[2]()
+    mid_steps[1]()
     wkv_steps[1]()
-    one_steps[2]()
     two_steps[1]()
     loads[5].wait()
     normalize(x_prompt, 0, 256)
+    one_steps[3]()
+    mid_steps[2]()
+    wq_steps[1]()
+    one_steps[4]()
     wkv_steps[2]()
+    mid_steps[3]()
     normalize(x_prompt, 256, 256)
-    one_steps[3]()
-    wkv_steps[3]()
     wq_steps[2]()
     loads[6].wait()
     normalize(x_resp, 0, 256)
-    one_steps[4]()
+    wkv_steps[3]()
     normalize(x_resp, 256, 256)
-    wkv_steps[4]()
+    mid_steps[4]()
     net.core_in(0)
     project(x_prompt, wkv_all, 256)
     keys, values = keys_values(s)
@@ -350,17 +365,20 @@
     two_steps[2]()
     kv_1()
     wq_steps[3]()
-    two_steps[3]()
     project(x_resp, wkv_all, 256)
     keys, values = keys_values(16)
     kv_own[:, 0:128] = keys
     kv_own[:, 128:256] = values
+    two_steps[3]()
     kv_2()
+    one_steps[5]()
     wq_steps[4]()
-    one_steps[5]()
+    net.core_in(1)
     two_steps[4]()
-    net.core_in(1)
-    project(x_resp, wq_all, Q_COLS)
+    kv_3()
+    mid_steps[5]()
+    project(x_resp, wq_all, Q_COLS, 0, 2)
+    project(x_resp, wq_all, Q_COLS, 2, 4)
     cosine, sine = angles(16)
     for h in range(Q_HEADS):
         cols = slice(h * HEAD, (h + 1) * HEAD)
@@ -368,7 +386,7 @@
         q_all[h] = (q * (math.log2(math.e) / math.sqrt(HEAD))).astype(BF16)
     reload = pltpu.make_async_copy(resp, x_resp, local.at[7])
     reload.start()
-    kv_3()
+    one_steps[6]()
     net.core_in(4)
 
     length = lengths[0]
@@ -433,43 +451,64 @@
         def _():
             att_second(h - 1)
 
+        @pl.when(h == 1)
+        def _():
+            two_steps[5]()
+            net.core_in(7)
+            mid_steps[6]()
+
+        @pl.when(h == 2)
+        def _():
+            net.core_in(2)
+
         @pl.when(h == 3)
         def _():
-            two_steps[5]()
-            one_steps[6]()
-
-        @pl.when(h == 4)
-        def _():
-            net.core_in(2)
             net.core_in(3)
+            two_steps[6]()
         return 0
 
     lax.fori_loop(0, Q_HEADS, head, 0)
-    att_second(Q_HEADS - 1)
     reload.wait()
-    for h in range(Q_HEADS):
-        att_third(h)
-    two_steps[6]()
     net.core_in(5)
 
     def out_copy(zz):
         cols = pl.ds(pl.multiple_of(zz * 1280, 1280), 1280)
         return pltpu.make_async_copy(x_prompt.at[:, cols], resid_out.at[:, cols], out_sem.at[zz])
 
-    def block(zz, _):
-        cols = pl.ds(pl.multiple_of(zz * 1280, 1280), 1280)
-        left = jnp.concatenate([attended[tt, h] for tt in range(4) for h in range(Q_HEADS)], 1)
+    def branch(zz, pieces):
+        left = jnp.concatenate([attended[tt, h] for tt, low, high in pieces for h in range(low, high)], 1)
         right = jnp.concatenate(
             [jnp.concatenate(
-                [buf for hh in range(2) for cc in range(2) for gg in range(2)
-                 for buf in (wo_one[cc, tt, zz, hh, gg], wo_two[cc, zz, hh, gg, tt])], 0)
-             for tt in range(4)], 1)
-        branch = lax.dot_general(left, right, NT, preferred_element_type=F32)
-        x_prompt[:, cols] = (x_resp[:, cols].astype(F32) + branch).astype(BF16)
+                [buf[:, low * HEAD:high * HEAD] for hh in range(2) for cc in range(2) for gg in range(2)
+                 for buf in (wo_one.at[cc, tt, zz, hh, gg], wo_mid.at[cc, tt, zz, hh, gg],
+                             wo_two.at[cc, zz, hh, gg, tt])], 0)
+             for tt, low, high in pieces], 1)
+        return lax.dot_general(left, right, NT, preferred_element_type=F32)
+
+    def first_pass(zz, _):
+        @pl.when(zz == 2)
+        def _():
+            att_second(Q_HEADS - 1)
+
+        cols = pl.ds(pl.multiple_of(zz * 1280, 1280), 1280)
+        term = branch(zz, [(t, 0, 4), (tm, 0, 4), (tp, 0, 4)])
+        x_prompt[:, cols] = (x_resp[:, cols].astype(F32) + term).astype(BF16)
+        return 0
+
+    lax.fori_loop(0, 4, first_pass, 0)
+    for h in range(Q_HEADS):
+        att_third(h)
+    net.core_in(8)
+    net.core_in(6)
+
+    def second_pass(zz, _):
+        cols = pl.ds(pl.multiple_of(zz * 1280, 1280), 1280)
+        term = branch(zz, [(t2, 0, 5), (t, 4, 5), (tm, 4, 5), (tp, 4, 5)])
+        x_prompt[:, cols] = (x_prompt[:, cols].astype(F32) + term).astype(BF16)
         out_copy(zz).start()
         return 0
 
-    lax.fori_loop(0, 4, block, 0)
+    lax.fori_loop(0, 4, second_pass, 0)
 
     net.finish()
     for h in range(Q_HEADS):
@@ -505,24 +544,25 @@
             pltpu.VMEM((2, 4, 2, 2, 160, Q_COLS), BF16),
             pltpu.VMEM((2, 4, 2, 2, 160, 256), BF16),
             pltpu.VMEM((2, 4, 4, 2, 2, ONE, Q_COLS), BF16),
+            pltpu.VMEM((2, 4, 4, 2, 2, MID, Q_COLS), BF16),
             pltpu.VMEM((2, 4, 2, 2, 4, TWO, Q_COLS), BF16),
             pltpu.VMEM((2, 4, 2, ROWS, 256), BF16),
             pltpu.VMEM((ROWS, 256), BF16),
             pltpu.VMEM((Q_HEADS, ROWS, HEAD), BF16),
             pltpu.VMEM((4, Q_HEADS, ROWS, HEAD), BF16),
             pltpu.VMEM((ROWS, Q_COLS), F32),
-            dma((90,)), dma((90,)), dma((70,)), dma((70,)), dma((Q_HEADS, 4)), dma((Q_HEADS, 4)), dma((8,)), dma((8,)),
+            dma((110,)), dma((110,)), dma((90,)), dma((90,)), dma((Q_HEADS, 4)), dma((Q_HEADS, 4)), dma((9,)), dma((4,)),
         ],
         compiler_params=pltpu.CompilerParams(
             collective_id=0, has_side_effects=True, vmem_limit_bytes=67000000),
         cost_estimate=pl.CostEstimate(flops=31_000_000_000, bytes_accessed=30_000_000, transcendentals=22_000_000),
     )(lengths, resp, prompt_hidden, norm_gain, wq, wk, wv, q_bias, k_bias, value_bias, wo_t,
       *tables)
-    block = pl.BlockSpec((64, WIDTH), lambda i: (i, 0))
+    block = pl.BlockSpec((128, WIDTH), lambda i: (i, 0))
     mixed = pl.pallas_call(
         finish_kernel,
         out_shape=jax.ShapeDtypeStruct((ROWS, WIDTH), BF16),
-        grid=(ROWS // 64,),
+        grid=(ROWS // 128,),
         in_specs=[smem, block, vmem],
         out_specs=block,
     )(lengths, resid, post_gain)

time: 136 us -> 127 us (0.934)
  Pallas kernels: 134 us -> 125 us
    pallas_call x1, Pallas kernels: 126 us -> 119 us  [on_device(): pl.pallas_call(kernel, out_shape=jax.ShapeDtypeStruct((ROWS, WIDTH), BF16...]
    pallas_call x1, Pallas kernels: 8.3 us -> 6.72 us  [on_device(): pl.pallas_call(finish_kernel, out_shape=jax.ShapeDtypeStruct((ROWS, WIDTH...]
where the time goes in v3:
time: 127 us; the launch traced here: 126 us
  Pallas kernels  125 us (98%)
    pallas_call x1, Pallas kernels, on_device(): pl.pallas_call(kernel, out_shape=jax.ShapeDtypeStruct((ROWS, WIDTH), BF16...  119 us
    pallas_call x1, Pallas kernels, on_device(): pl.pallas_call(finish_kernel, out_shape=jax.ShapeDtypeStruct((ROWS, WIDTH...  6.72 us

profile of v3, /device:TPU:1, one launch (start us, length us, event | category | flops | bytes accessed | tf_op | source)
XLA Modules:
  0.0 126.0 jit_solution(14269276031436064337)
XLA Ops:
  0.7 118.6 %shard_map.154.resid = bf16[512,5120]{1,0:T(8,128)(2,1)} custom-call(s32[1]{0:T(128)S(6)} %copy.17.lengths, bf16[512,5120]{1,0:T(8,128)(2,1)} %bitcast.2, bf16[512,5120]{1,0:T(8,128)(2,1)} %prompt.1, bf16[5120]{0:T(1024)(128)(2,1)} %gain.2, bf16[320,640]{1,0:T(8,128)(2,1)} %wq.1, bf16[320,128]{1,0:T(8,128)(2,1)} %wk.1, bf16[320,128]{1,0:T(8,128)(2,1)} %wv.1, ...), custom_call_target="tpu_custom_call" | custom-call | flops 31000000512 | bytes 30000000 | tf_op jit(solution)/shard_map/pallas_call | solution.py:536
  119.2 6.7 %shard_map.155 = bf16[512,5120]{1,0:T(8,128)(2,1)} custom-call(s32[1]{0:T(128)S(6)} %copy.17.lengths, bf16[512,5120]{1,0:T(8,128)(2,1)} %shard_map.154.resid, bf16[5120]{0:T(1024)(128)(2,1)} %gain.3), custom_call_target="tpu_custom_call" | custom-call | tf_op jit(solution)/shard_map/pallas_call | solution.py:562
